TPU v7x, 256 devices: a whole 4x4x8 slice. The times are simulated.
256 devices in a mesh: grp: 64 (over y_lo, x, z), rep: 4 (over y_hi, core).
Axes of the slice: x: 4, y: 4 (y_hi: 2, y_lo: 2; y = y_hi * 2 + y_lo), z: 8, core: 2. Of those that a mesh axis runs over, the one named last changes fastest.
Arguments:
- deviation: float32 [256, 6, 256], P('grp'), may hold values from -6 to 6
- source: float32 [256, 6, 256], P('grp'), may hold values from -6 to 6
- lifetime: float32 [256, 256], P('grp'), may hold values from 0.3 to 3
- rates: float32 [256, 20, 256, 256], P('grp', 'rep'), may hold values from -0.15625 to 0.15625
- partner: int32 [256, 20], P('grp', 'rep'), may hold values from 192 to 255, as said below
- count: int32 [256, 4], P('grp', 'rep'), may hold values from 1 to 5, as said below
Outputs:
- new_deviation: float32 [256, 6, 256], P('grp')
Inputs may be any that keep to these rules, and one draw needn't show every extreme that they name: Every partner is a phonon block. Slots k < count of a share are live, the others are ignored.
All inputs are finite; a program needn't handle non-finite values.
Results may differ from a plain program's by a relative error of at most 0.0003.
Values sent between devices are 32-bit elements; how exact they have to be, the bound alone decides.
No kernel may reach another device: no remote copies, remote signals or barrier semaphores. Data moves between devices by JAX's collectives and lax.ppermute only.
A program may use at most 64 MiB of HBM per device.

v0:
```python
import jax
import jax.numpy as jnp
from jax import lax
from jax.sharding import PartitionSpec as P


def on_device(deviation, source, lifetime, rates, partner, count):
    blocks = deviation.shape[0]
    groups = lax.axis_size("grp")
    owners = groups // 4
    phonon_blocks = owners * blocks
    electron_blocks = 3 * owners * blocks
    position = lax.axis_index("grp")
    is_electron = (position < 3 * owners).astype(jnp.float32)
    tail = deviation.shape[1:]
    everything = lax.all_gather(deviation, "grp", axis=0, tiled=True)
    phonon = everything[electron_blocks:]
    slot_count = rates.shape[1]
    target = partner - electron_blocks
    live_count = count[:, 0]
    columns = lax.iota(jnp.int32, phonon_blocks)

    def visit_slot(number, totals):
        forward, drag_sum = totals
        weights = lax.dynamic_index_in_dim(rates, number, 1, keepdims=False)
        chosen = lax.dynamic_index_in_dim(target, number, 1, keepdims=False)
        live_mask = (number < live_count).astype(jnp.float32)
        picked = jnp.take(phonon, chosen, axis=0)
        forward = forward + live_mask[:, None, None] * jnp.einsum(
            "bij,bcj->bci", weights, picked, precision=lax.Precision.HIGHEST
        )
        spread = jnp.einsum("bij,bci->bcj", weights, deviation, precision=lax.Precision.HIGHEST)
        spread = (live_mask * is_electron)[:, None, None] * spread
        onehot = (chosen[:, None] == columns[None, :]).astype(jnp.float32)
        drag_sum = drag_sum + jnp.einsum(
            "bp,bx->px", onehot, spread.reshape(blocks, -1), precision=lax.Precision.HIGHEST
        )
        return (forward, drag_sum)

    initial = (
        jnp.zeros(deviation.shape, jnp.float32),
        jnp.zeros((phonon_blocks, tail[0] * tail[1]), jnp.float32),
    )
    forward, drag_sum = lax.fori_loop(0, slot_count, visit_slot, initial)
    drag_rows = drag_sum.reshape((phonon_blocks,) + tail)
    leading = jnp.zeros((electron_blocks,) + tail, jnp.float32)
    partial_value = jnp.concatenate([leading, drag_rows], axis=0)
    own_drag = lax.psum_scatter(partial_value, "grp", scatter_dimension=0, tiled=True)
    summed = lax.psum(forward + own_drag, "rep")
    return source + lifetime[:, None, :] * summed


def solution(mesh):
    placed = (
        P("grp", None, None),
        P("grp", None, None),
        P("grp", None),
        P("grp", "rep", None, None),
        P("grp", "rep"),
        P("grp", "rep"),
    )
    return jax.shard_map(
        on_device, mesh=mesh, in_specs=placed, out_specs=P("grp", None, None), check_vma=False
    )
```

profile of v0, /device:TPU:1, one launch (start us, length us, event | category | flops | bytes accessed | tf_op | source)
XLA Modules:
  0.0 684.3 jit_solution(6879271114496984113)
XLA Ops:
  6.5 1.4 copy.19
  8.0 0.8 copy.18
  8.8 260.1 %all-gather.2.cloned.1.call-done = f32[256,6,256]{2,1,0:T(8,128)} async-done(((f32[4,6,256]{2,1,0:T(8,128)}), f32[256,6,256]{2,1,0:T(8,128)}) %all-gather.2.cloned.1.call-update) | async-done | bytes 1572880 | tf_op jit(solution)/shard_map/all_gather | solution.py:16
  268.8 1.1 slice.6
  269.9 32.6 %while.16 = (s32[]{:T(128)}, f32[4,6,256]{2,1,0:T(8,128)S(1)}, f32[64,1536]{1,0:T(8,128)S(1)}, s32[4]{0:T(128)}, s32[4,5]{0,1:T(8,128)S(1)}, /*index=5*/f32[64,6...) while((s32[]{:T(128)}, f32[4,6,256]{2,1,0:T(8,128)S(1)}, ...), condition=%wide.region_1.2_spmd.clone, body=%wide.region_0.1_spmd.clone.sunk | while | flops 42695976 | bytes 3143012 | solution.py:44
  269.9 0.7 compare_select_fusion.4
  270.6 1.9 fusion.32
  273.0 0.6 gather_fusion
  273.6 0.7 compare_convert_fusion.2
  274.2 2.2 fusion.31
  276.4 0.7 compare_select_fusion.4
  277.1 1.9 fusion.32
  279.6 0.6 gather_fusion
  280.1 0.7 compare_convert_fusion.2
  280.8 2.2 fusion.31
  283.0 0.7 compare_select_fusion.4
  283.6 1.9 fusion.32
  286.6 0.7 compare_convert_fusion.2
  287.3 2.2 fusion.31
  289.5 0.7 compare_select_fusion.4
  290.2 1.9 fusion.32
  293.2 0.7 compare_convert_fusion.2
  293.8 2.2 fusion.31
  296.0 0.7 compare_select_fusion.4
  296.7 1.9 fusion.32
  299.7 0.7 compare_convert_fusion.2
  300.4 2.2 fusion.31
  302.7 1.5 concatenate.3
  304.2 308.5 %reduce-scatter.2.cloned.1.call-done = f32[4,6,256]{2,1,0:T(8,128)} async-done(((f32[256,6,256]{2,1,0:T(8,128)}), f32[4,6,256]{2,1,0:T(8,128)}) %reduce-scatter.2.cloned.1.call-update) | async-done | bytes 24592 | tf_op jit(solution)/shard_map/reduce_scatter | solution.py:48
  612.7 0.8 add.63
  613.5 63.4 %psum.7 = f32[4,6,256]{2,1,0:T(8,128)S(1)} all-reduce(f32[4,6,256]{2,1,0:T(8,128)S(1)} %add.63), channel_id=1, replica_groups=mesh['grp'=64,'rep'=4] {'rep'}, use_global_device_ids=true, to_apply=%region_3.4 | all-reduce | flops 6144 | bytes 49152 | tf_op jit(solution)/shard_map/psum | solution.py:49
  676.8 0.6 copy.23
  (41 shorter events, 4.6 us)
Async XLA Ops:
  6.5 262.3 %all-gather.2.cloned.1.call-start = ((), (), s32[]{:S(2)}) async-start(), calls=%async_computation.1 | async-start | bytes 2129920 | tf_op jit(solution)/shard_map/all_gather | solution.py:16
  7.9 604.8 %reduce-scatter.2.cloned.1.call-start = ((), (), s32[]{:S(2)}) async-start(), calls=%async_computation.2 | async-start | bytes 2129920 | tf_op jit(solution)/shard_map/reduce_scatter | solution.py:48
  302.5 374.3 %copy-start = (f32[4,6,256]{2,0,1:T(4,128)S(1)}, f32[4,6,256]{2,0,1:T(4,128)}, u32[]{:S(2)}) copy-start(f32[4,6,256]{2,0,1:T(4,128)} %param.9) | copy-start | bytes 73732
  302.6 374.3 %copy-start.1 = (f32[4,256]{1,0:T(4,128)S(1)}, f32[4,256]{1,0:T(4,128)}, u32[]{:S(2)}) copy-start(f32[4,256]{1,0:T(4,128)} %param.10) | copy-start | bytes 12292
Sparse Core Ops, SparseCore 0:
  9.1 259.6 all-gather.1
  304.3 308.3 reduce-scatter.1
where the time goes:
time: 685 us; the launch traced here: 684 us
  waiting for transfers between devices  569 us (83%)
  blocking collectives  63.4 us (9%)
  matrix products  22.8 us (3%)
  between operations  13.5 us (2%)
  local copies, waits for them, and re-layouts  8.27 us (1%)
  other arithmetic  7.54 us (1%)
    reduce_scatter x1, waiting for transfers between devices, on_device(): lax.psum_scatter(partial_value, 'grp', scatter_dimension=0, tiled=True)  309 us
    all_gather x1, waiting for transfers between devices, on_device(): everything = lax.all_gather(deviation, 'grp', axis=0, tiled=True)  260 us
    psum x1, blocking collectives, on_device(): summed = lax.psum(forward + own_drag, 'rep')  63.4 us
  transfers between devices with their start and end apart: 2, of which 2 were waited for; matrix products, arithmetic and copies ran while one was open for 0% of the time, Pallas kernels for 0%

commit v1 on v0

v1 whole, which is shorter than its diff:
```python
import jax
import jax.numpy as jnp
from jax import lax
from jax.experimental import pallas as pl
from jax.experimental.pallas import tpu as pltpu
from jax.sharding import PartitionSpec as P

Y_LO, X_HIGH, Y_HI, CORE = 128, 64, 2, 1
DEVICES = 256
BLOCKS, SLOTS, COMPONENTS, STATES, HALF = 4, 5, 6, 256, 128
PHONON = 64
FIRST_PHONON = 192
ROWS = BLOCKS * COMPONENTS
OWNERS = PHONON // BLOCKS
QUARTERS = [[quarter * OWNERS + owner for owner in range(OWNERS)] for quarter in range(4)]


def swap(value, bit):
    return lax.ppermute(value, ("grp", "rep"), [(i, i ^ bit) for i in range(DEVICES)])


def push(value, bit, towards, also=0):
    pairs = [
        (i, i ^ bit) for i in range(DEVICES) if ((i ^ bit) & bit != 0) == towards and i & also == also
    ]
    return lax.ppermute(value, ("grp", "rep"), pairs)


def split(value):
    high = value.astype(jnp.bfloat16)
    low = (value - high.astype(jnp.float32)).astype(jnp.bfloat16)
    return high, low


def stack_split(value):
    padded = jnp.concatenate([value, jnp.zeros((2, value.shape[1]), jnp.float32)], axis=0)
    high, low = split(padded)
    both = jnp.concatenate([high.astype(jnp.float32), low.astype(jnp.float32)], axis=0)
    return high, both.astype(jnp.bfloat16)


def product(high, both, weights, contract):
    dims = (((1,), (contract,)), ((), ()))
    rates_high, rates_low = split(weights)
    main = lax.dot_general(both, rates_high, dims, preferred_element_type=jnp.float32)
    rest = lax.dot_general(high, rates_low, dims, preferred_element_type=jnp.float32)
    return main[:8] + main[8:] + rest


def fetch(rates, held, sems, block, slot):
    return pltpu.make_async_copy(
        rates.at[block, slot], held.at[block * SLOTS + slot], sems.at[block * SLOTS + slot]
    )


def start_fetches(count, rates, held, sems):
    for block in range(BLOCKS):

        @pl.loop(0, count[block])
        def _(slot):
            fetch(rates, held, sems, block, slot).start()


def spread_kernel(count, target, deviation, rates, out, held, sems):
    start_fetches(count, rates, held, sems)
    out[...] = jnp.zeros_like(out)
    for block in range(BLOCKS):
        high, both = stack_split(deviation[block])

        @pl.loop(0, count[block])
        def _(slot):
            fetch(rates, held, sems, block, slot).wait()
            value = product(high, both, held[block * SLOTS + slot], 0)
            row = target[block * SLOTS + slot] * COMPONENTS
            out[0, pl.ds(row, COMPONENTS), :] += value[:COMPONENTS, :HALF]
            out[1, pl.ds(row, COMPONENTS), :] += value[:COMPONENTS, HALF:]


def forward_kernel(count, target, phonon, rates, out, held, sems):
    start_fetches(count, rates, held, sems)
    for block in range(BLOCKS):

        def visit(slot, total):
            fetch(rates, held, sems, block, slot).wait()
            row = target[block * SLOTS + slot] * COMPONENTS
            picked = jnp.concatenate(
                [phonon[0, pl.ds(row, COMPONENTS), :], phonon[1, pl.ds(row, COMPONENTS), :]], axis=1
            )
            high, both = stack_split(picked)
            return total + product(high, both, held[block * SLOTS + slot], 1)

        total = lax.fori_loop(0, count[block], visit, jnp.zeros((8, STATES), jnp.float32))
        for half in range(2):
            out[half, block * COMPONENTS : (block + 1) * COMPONENTS, :] = total[
                :COMPONENTS, half * HALF : (half + 1) * HALF
            ]


def rate_kernel(body, name, rows):
    smem = pl.BlockSpec(memory_space=pltpu.SMEM)
    vmem = pl.BlockSpec(memory_space=pltpu.VMEM)
    return pl.pallas_call(
        body,
        name=name,
        out_shape=jax.ShapeDtypeStruct((2, rows, HALF), jnp.float32),
        in_specs=[smem, smem, vmem, pl.BlockSpec(memory_space=pl.ANY)],
        out_specs=vmem,
        scratch_shapes=[
            pltpu.VMEM((BLOCKS * SLOTS, STATES, STATES), jnp.float32),
            pltpu.SemaphoreType.DMA((BLOCKS * SLOTS,)),
        ],
        compiler_params=pltpu.CompilerParams(vmem_limit_bytes=24 * 1024 * 1024),
        cost_estimate=pl.CostEstimate(
            flops=6 * BLOCKS * SLOTS * 8 * STATES * STATES,
            bytes_accessed=BLOCKS * SLOTS * STATES * STATES * 4,
            transcendentals=0,
        ),
    )


def on_device(deviation, source, lifetime, rates, partner, count):
    grp = lax.axis_index("grp")
    core = lax.axis_index("rep") % 2
    is_phonon = grp >= 3 * OWNERS
    target = (partner - FIRST_PHONON).reshape(-1)
    live = count[:, 0]

    def half_of(value):
        return lax.dynamic_index_in_dim(value, core, 0, keepdims=False)

    def other_of(value):
        return lax.dynamic_index_in_dim(value, 1 - core, 0, keepdims=False)

    def both_halves(mine, other):
        return jnp.stack([jnp.where(core == 0, mine, other), jnp.where(core == 0, other, mine)])

    own = lax.dynamic_slice_in_dim(deviation, core * HALF, HALF, 2).reshape(ROWS, HALF)
    from_phonon = push(own, Y_LO, False, also=Y_LO + X_HIGH)
    at_x_high = jnp.where(is_phonon, own, from_phonon)
    from_x_high = push(at_x_high, X_HIGH, False)
    has_x_high = (grp // OWNERS) % 2 == 1
    carried = jnp.where(has_x_high, at_x_high, from_x_high)

    spread_live = jnp.where(is_phonon, 0, live)
    spread = rate_kernel(spread_kernel, "spread", PHONON * COMPONENTS)(
        spread_live, target, deviation, rates
    )
    drag = half_of(spread) + swap(other_of(spread), CORE)

    parcel = jnp.concatenate(
        [drag.reshape(OWNERS, ROWS, HALF), jnp.broadcast_to(carried, (OWNERS, ROWS, HALF))], axis=1
    )
    arrived = lax.all_to_all(parcel, "grp", 0, 0, axis_index_groups=QUARTERS, tiled=True)
    drag = arrived[:, :ROWS].sum(0)
    phonon_half = arrived[:, ROWS:].reshape(PHONON * COMPONENTS, HALF)

    phonon = both_halves(phonon_half, swap(phonon_half, CORE))
    forward = rate_kernel(forward_kernel, "forward", ROWS)(live, target, phonon, rates)
    forward = half_of(forward) + swap(other_of(forward), CORE)

    drag = drag + push(drag, Y_LO, True)
    drag = drag + push(drag, X_HIGH, True)
    total = forward + jnp.where(is_phonon, drag, 0.0)
    total = total + swap(total, Y_HI)
    halves = both_halves(total, swap(total, CORE)).reshape(2, BLOCKS, COMPONENTS, HALF)
    summed = jnp.concatenate([halves[0], halves[1]], axis=-1)
    return source + lifetime[:, None, :] * summed


def solution(mesh):
    placed = (
        P("grp", None, None),
        P("grp", None, None),
        P("grp", None),
        P("grp", "rep", None, None),
        P("grp", "rep"),
        P("grp", "rep"),
    )
    return jax.shard_map(
        on_device, mesh=mesh, in_specs=placed, out_specs=P("grp", None, None), check_vma=False
    )
```

time: 685 us -> 60.8 us (0.09)
  waiting for transfers between devices: 569 us -> 4.85 us
  blocking collectives: 63.4 us -> 18.1 us
  starting transfers between devices: 0.04 us -> 23.2 us
  matrix products: 22.8 us -> 0 us
  between operations: 13.5 us -> 0.18 us
    reduce_scatter x1 -> x0, waiting for transfers between devices: 309 us -> none  [on_device(): lax.psum_scatter(partial_value, 'grp', scatter_dimension=0, tiled=True)]
    all_gather x1 -> x0, waiting for transfers between devices: 260 us -> none  [on_device(): everything = lax.all_gather(deviation, 'grp', axis=0, tiled=True)]
    psum x1 -> x0, blocking collectives: 63.4 us -> none  [on_device(): summed = lax.psum(forward + own_drag, 'rep')]
    ppermute x0 -> x9, starting transfers between devices: none -> 23.2 us  [the longest x5 14.1 us: swap(): lax.ppermute(value, ('grp', 'rep'), [(i, i ^ bit) for i in range(DEVICES)])]
    dot_general x15 -> x0, matrix products: 22.8 us -> none  [the longest x5 10.9 us: visit_slot(): jnp.einsum('bij,bcj->bci', weights, picked, precision=lax.Precision.HIGHEST)]
    all_to_all x0 -> x1, blocking collectives: none -> 18.1 us  [on_device(): lax.all_to_all(parcel, 'grp', 0, 0, axis_index_groups=QUARTERS, tiled=True)]
  transfers between devices with their start and end apart: 2 -> 9, of which waited for: 2 -> 5; matrix products, arithmetic and copies ran while one was open for 0% -> 4% of each run, Pallas kernels for 0% -> 9%
where the time goes in v1:
time: 60.8 us; the launch traced here: 60.5 us
  starting transfers between devices  23.2 us (38%)
  blocking collectives  18.1 us (30%)
  local copies, waits for them, and re-layouts  7.2 us (12%)
  Pallas kernels  5.48 us (9%)
  waiting for transfers between devices  4.85 us (8%)
  other arithmetic  1.56 us (3%)
    all_to_all x1, blocking collectives, on_device(): lax.all_to_all(parcel, 'grp', 0, 0, axis_index_groups=QUARTERS, tiled=True)  18.1 us
    ppermute x5, starting transfers between devices, swap(): lax.ppermute(value, ('grp', 'rep'), [(i, i ^ bit) for i in range(DEVICES)])  14.1 us
    ppermute x4, starting transfers between devices, push(): return lax.ppermute(value, ('grp', 'rep'), pairs)  9.05 us
    unnamed x11, local copies, waits for them, and re-layouts  5.72 us
    pallas_call x1, Pallas kernels, on_device(): rate_kernel(forward_kernel, 'forward', ROWS)(live, target, phonon, rates)  2.89 us
    ppermute x5, waiting for transfers between devices, swap(): lax.ppermute(value, ('grp', 'rep'), [(i, i ^ bit) for i in range(DEVICES)])  2.75 us
    pallas_call x1, Pallas kernels, on_device(): rate_kernel(spread_kernel, 'spread', PHONON * COMPONENTS)  2.59 us
    ppermute x4, waiting for transfers between devices, push(): return lax.ppermute(value, ('grp', 'rep'), pairs)  2.1 us
  transfers between devices with their start and end apart: 9, of which 5 were waited for; matrix products, arithmetic and copies ran while one was open for 4% of the time, Pallas kernels for 9%

profile of v1, /device:TPU:1, one launch (start us, length us, event | category | flops | bytes accessed | tf_op | source)
XLA Modules:
  0.0 60.5 jit_solution(12316303661492336460)
XLA Ops:
  0.0 0.7 %constant_dynamic-slice_fusion = f32[4,6,128]{2,0,1:T(4,128)S(1)} fusion(f32[4,6,256]{2,0,1:T(4,128)} %param.6, s32[]{:T(128)S(6)} %select_n.89), kind=kLoop, calls=%fused_computation.16 | loop fusion | bytes 24580 | tf_op jit(solution)/shard_map/dynamic_slice | solution.py:137
  0.7 0.7 %collective-permute-start.1 = (f32[24,128]{1,0:T(8,128)S(1)}, f32[24,128]{1,0:T(8,128)S(1)}, u32[]{:S(2)}, u32[]{:S(2)}) collective-permute-start(f32[24,128]{1,0:T(8,128)S(1)} %reshape.22), channel_id=1, source_target_pairs={{192,64},{193,65},{194,66},{195,67},{196,68},{197,69},{198,70},{19... | collective-permute-start | bytes 36872 | tf_op jit(solution)/shard_map/ppermute | solution.py:26
  1.4 0.7 %broadcast_add_fusion = s32[4,5]{1,0:T(4,128)S(1)} fusion(s32[4,5]{1,0:T(4,128)} %param.10), kind=kLoop, calls=%fused_computation.17 | loop fusion | flops 20 | bytes 160 | tf_op jit(solution)/shard_map/sub | solution.py:125
  2.1 0.7 %broadcast_select_fusion.4.count = s32[4]{0:T(128)S(1)} fusion(pred[]{:T(512)S(6)} %ge.3, s32[4,1]{0,1:T(1,128)} %param.11), kind=kLoop, calls=%fused_computation.18 | loop fusion | flops 4 | bytes 33 | tf_op jit(solution)/shard_map/jit(_where)/select_n | solution.py:144
  2.7 0.7 %copy.8.deviation = f32[4,6,256]{2,1,0:T(8,128)S(1)} copy(f32[4,6,256]{2,0,1:T(4,128)} %param.6) | data formatting | bytes 49152 | tf_op args[0]
  3.5 0.1 reshape.20.target
  3.6 2.5 %copy-done = f32[4,5,256,256]{3,2,1,0:T(8,128)S(1)} copy-done((f32[4,5,256,256]{3,2,1,0:T(8,128)S(1)}, f32[4,5,256,256]{3,2,1,0:T(8,128)}, u32[]{:S(2)}) %copy-start) | copy-done | bytes 5242904
  6.0 2.6 %spread.1 = f32[2,384,128]{2,1,0:T(8,128)S(1)} custom-call(s32[4]{0:T(128)S(1)} %broadcast_select_fusion.4.count, s32[20]{0:T(128)S(1)} %reshape.20.target, f32[4,6,256]{2,1,0:T(8,128)S(1)} %copy.8.deviation, f32[4,5,256,256]{3,2,1,0:T(8,128)S(1)} %copy-done), custom_call_target="tpu_custom_call" | custom-call | flops 62914560 | bytes 5242880 | tf_op jit(solution)/shard_map/spread/pallas_call | solution.py:145
  8.6 0.0 collective-permute-done.1
  8.7 1.3 %collective-permute-start.2 = (f32[24,128]{1,0:T(8,128)S(1)}, f32[24,128]{1,0:T(8,128)S(1)}, u32[]{:S(2)}, u32[]{:S(2)}) collective-permute-start(f32[24,128]{1,0:T(8,128)S(1)} %broadcast_select_fusion), channel_id=1, source_target_pairs={{64,0},{65,1},{66,2},{67,3},{68,4},{69,5},{70,6},{71,7},{72,8},{73... | collective-permute-start | bytes 36872 | tf_op jit(solution)/shard_map/ppermute | solution.py:26
  10.0 3.3 %collective-permute-start = (f32[384,128]{1,0:T(8,128)S(1)}, f32[384,128]{1,0:T(8,128)S(1)}, u32[]{:S(2)}, u32[]{:S(2)}) collective-permute-start(f32[384,128]{1,0:T(8,128)S(1)} %dynamic-slice_bitcast_fusion), channel_id=1, source_target_pairs={{0,1},{1,0},{2,3},{3,2},{4,5},{5,4},{6,7},{7,6},{8,9},{9,8},{10,11... | collective-permute-start | bytes 589832 | tf_op jit(solution)/shard_map/ppermute | solution.py:19
  13.3 1.3 %collective-permute-done.2 = f32[24,128]{1,0:T(8,128)S(1)} collective-permute-done((f32[24,128]{1,0:T(8,128)S(1)}, f32[24,128]{1,0:T(8,128)S(1)}, u32[]{:S(2)}, u32[]{:S(2)}) %collective-permute-start.2) | collective-permute-done | bytes 12320 | tf_op jit(solution)/shard_map/ppermute | solution.py:26
  14.6 0.0 collective-permute-done
  14.7 18.1 %all_to_all.5 = f32[16,48,128]{2,1,0:T(8,128)S(1)} all-to-all(f32[16,48,128]{2,1,0:T(8,128)S(1)} %pad_maximum_fusion), channel_id=1, replica_groups={{0,4,8,12,16,20,24,28,32,36,40,44,48,52,56,60},{64,68,72,76,80,84,88,92..., dimensions={0} | all-to-all | bytes 786432 | tf_op jit(solution)/shard_map/all_to_all | solution.py:153
  32.8 5.1 %collective-permute-start.3 = (f32[384,128]{1,0:T(8,128)S(1)}, f32[384,128]{1,0:T(8,128)S(1)}, u32[]{:S(2)}, u32[]{:S(2)}) collective-permute-start(f32[384,128]{1,0:T(8,128)S(1)} %bitcast.21), channel_id=1, source_target_pairs={{0,1},{1,0},{2,3},{3,2},{4,5},{5,4},{6,7},{7,6},{8,9},{9,8},{10,11... | collective-permute-start | bytes 589832 | tf_op jit(solution)/shard_map/ppermute | solution.py:19
  37.9 3.9 %collective-permute-start.5 = (f32[24,128]{1,0:T(8,128)S(1)}, f32[24,128]{1,0:T(8,128)S(1)}, u32[]{:S(2)}, u32[]{:S(2)}) collective-permute-start(f32[24,128]{1,0:T(8,128)S(1)} %get-tuple-element.5), channel_id=1, source_target_pairs={{0,128},{1,129},{2,130},{3,131},{4,132},{5,133},{6,134},{7,135},{8... | collective-permute-start | bytes 36872 | tf_op jit(solution)/shard_map/ppermute | solution.py:26
  41.8 0.8 %collective-permute-done.5 = f32[24,128]{1,0:T(8,128)S(1)} collective-permute-done((f32[24,128]{1,0:T(8,128)S(1)}, f32[24,128]{1,0:T(8,128)S(1)}, u32[]{:S(2)}, u32[]{:S(2)}) %collective-permute-start.5) | collective-permute-done | bytes 12320 | tf_op jit(solution)/shard_map/ppermute | solution.py:26
  42.6 3.2 %collective-permute-start.6 = (f32[24,128]{1,0:T(8,128)S(1)}, f32[24,128]{1,0:T(8,128)S(1)}, u32[]{:S(2)}, u32[]{:S(2)}) collective-permute-start(f32[24,128]{1,0:T(8,128)S(1)} %add.51), channel_id=1, source_target_pairs={{0,64},{1,65},{2,66},{3,67},{4,68},{5,69},{6,70},{7,71},{8,72},{9,... | collective-permute-start | bytes 36872 | tf_op jit(solution)/shard_map/ppermute | solution.py:26
  45.8 0.0 collective-permute-done.3
  45.9 0.1 pad_maximum_fusion.1.phonon
  45.9 0.0 copy-start.1
  45.9 2.5 %copy-done.1 = f32[4,5,256,256]{3,2,1,0:T(8,128)S(1)} copy-done((f32[4,5,256,256]{3,2,1,0:T(8,128)S(1)}, f32[4,5,256,256]{3,2,1,0:T(8,128)}, u32[]{:S(2)}) %copy-start.1) | copy-done | bytes 5242904
  48.4 2.9 %forward.1 = f32[2,24,128]{2,1,0:T(8,128)S(1)} custom-call(s32[4]{0:T(128)S(1)} %bitcast.20, s32[20]{0:T(128)S(1)} %reshape.20.target, f32[2,384,128]{2,1,0:T(8,128)S(1)} %pad_maximum_fusion.1.phonon, f32[4,5,256,256]{3,2,1,0:T(8,128)S(1)} %copy-done.1), custom_call_target="tpu_custom_call" | custom-call | flops 62914560 | bytes 5242880 | tf_op jit(solution)/shard_map/forward/pallas_call | solution.py:158
  51.3 1.2 %collective-permute-start.4 = (f32[24,128]{1,0:T(8,128)S(1)}, f32[24,128]{1,0:T(8,128)S(1)}, u32[]{:S(2)}, u32[]{:S(2)}) collective-permute-start(f32[24,128]{1,0:T(8,128)S(1)} %dynamic-slice_bitcast_fusion.1), channel_id=1, source_target_pairs={{0,1},{1,0},{2,3},{3,2},{4,5},{5,4},{6,7},{7,6},{8,9},{9,8},{10,11... | collective-permute-start | bytes 36872 | tf_op jit(solution)/shard_map/ppermute | solution.py:19
  52.6 0.0 collective-permute-done.6
  52.6 0.8 %collective-permute-done.4 = f32[24,128]{1,0:T(8,128)S(1)} collective-permute-done((f32[24,128]{1,0:T(8,128)S(1)}, f32[24,128]{1,0:T(8,128)S(1)}, u32[]{:S(2)}, u32[]{:S(2)}) %collective-permute-start.4) | collective-permute-done | bytes 12320 | tf_op jit(solution)/shard_map/ppermute | solution.py:19
  53.4 3.2 %collective-permute-start.7 = (f32[24,128]{1,0:T(8,128)S(1)}, f32[24,128]{1,0:T(8,128)S(1)}, u32[]{:S(2)}, u32[]{:S(2)}) collective-permute-start(f32[24,128]{1,0:T(8,128)S(1)} %fusion.1), channel_id=1, source_target_pairs={{0,2},{1,3},{2,0},{3,1},{4,6},{5,7},{6,4},{7,5},{8,10},{9,11},{10,... | collective-permute-start | bytes 36872 | tf_op jit(solution)/shard_map/ppermute | solution.py:19
  56.6 1.1 %collective-permute-done.7 = f32[24,128]{1,0:T(8,128)S(1)} collective-permute-done((f32[24,128]{1,0:T(8,128)S(1)}, f32[24,128]{1,0:T(8,128)S(1)}, u32[]{:S(2)}, u32[]{:S(2)}) %collective-permute-start.7) | collective-permute-done | bytes 12320 | tf_op jit(solution)/shard_map/ppermute | solution.py:19
  57.7 1.3 %collective-permute-start.8 = (f32[24,128]{1,0:T(8,128)S(1)}, f32[24,128]{1,0:T(8,128)S(1)}, u32[]{:S(2)}, u32[]{:S(2)}) collective-permute-start(f32[24,128]{1,0:T(8,128)S(1)} %add.54), channel_id=1, source_target_pairs={{0,1},{1,0},{2,3},{3,2},{4,5},{5,4},{6,7},{7,6},{8,9},{9,8},{10,11... | collective-permute-start | bytes 36872 | tf_op jit(solution)/shard_map/ppermute | solution.py:19
  59.0 0.8 %collective-permute-done.8 = f32[24,128]{1,0:T(8,128)S(1)} collective-permute-done((f32[24,128]{1,0:T(8,128)S(1)}, f32[24,128]{1,0:T(8,128)S(1)}, u32[]{:S(2)}, u32[]{:S(2)}) %collective-permute-start.8) | collective-permute-done | bytes 12320 | tf_op jit(solution)/shard_map/ppermute | solution.py:19
  59.8 0.0 copy-done.3
  59.9 0.6 %copy.11 = f32[4,6,256]{2,0,1:T(4,128)} copy(f32[4,6,256]{2,1,0:T(8,128)S(1)} %fusion) | data formatting | bytes 49152 | tf_op jit(solution)/shard_map/add | solution.py:167
  (24 shorter events, 0.2 us)
Async XLA Ops:
  0.7 7.9 %collective-permute-start.1 = (f32[24,128]{1,0:T(8,128)S(1)}, f32[24,128]{1,0:T(8,128)S(1)}, u32[]{:S(2)}, u32[]{:S(2)}) collective-permute-start(f32[24,128]{1,0:T(8,128)S(1)} %reshape.22), channel_id=1, source_target_pairs={{192,64},{193,65},{194,66},{195,67},{196,68},{197,69},{198,70},{19... | collective-permute-start | bytes 36872 | tf_op jit(solution)/shard_map/ppermute | solution.py:26
  3.6 2.5 %copy-start = (f32[4,5,256,256]{3,2,1,0:T(8,128)S(1)}, f32[4,5,256,256]{3,2,1,0:T(8,128)}, u32[]{:S(2)}) copy-start(f32[4,5,256,256]{3,2,1,0:T(8,128)} %rates.3) | copy-start | bytes 15728644
  6.0 39.9 %copy-start.2 = (s32[4,1]{0,1:T(1,128)S(1)}, s32[4,1]{0,1:T(1,128)}, u32[]{:S(2)}) copy-start(s32[4,1]{0,1:T(1,128)} %param.11) | copy-start | bytes 52
  8.7 5.9 %collective-permute-start.2 = (f32[24,128]{1,0:T(8,128)S(1)}, f32[24,128]{1,0:T(8,128)S(1)}, u32[]{:S(2)}, u32[]{:S(2)}) collective-permute-start(f32[24,128]{1,0:T(8,128)S(1)} %broadcast_select_fusion), channel_id=1, source_target_pairs={{64,0},{65,1},{66,2},{67,3},{68,4},{69,5},{70,6},{71,7},{72,8},{73... | collective-permute-start | bytes 36872 | tf_op jit(solution)/shard_map/ppermute | solution.py:26
  10.0 4.6 %collective-permute-start = (f32[384,128]{1,0:T(8,128)S(1)}, f32[384,128]{1,0:T(8,128)S(1)}, u32[]{:S(2)}, u32[]{:S(2)}) collective-permute-start(f32[384,128]{1,0:T(8,128)S(1)} %dynamic-slice_bitcast_fusion), channel_id=1, source_target_pairs={{0,1},{1,0},{2,3},{3,2},{4,5},{5,4},{6,7},{7,6},{8,9},{9,8},{10,11... | collective-permute-start | bytes 589832 | tf_op jit(solution)/shard_map/ppermute | solution.py:19
  14.6 45.2 %copy-start.3 = (f32[4,6,256]{2,0,1:T(4,128)S(1)}, f32[4,6,256]{2,0,1:T(4,128)}, u32[]{:S(2)}) copy-start(f32[4,6,256]{2,0,1:T(4,128)} %param.7) | copy-start | bytes 73732
  14.6 45.2 %copy-start.4 = (f32[4,256]{1,0:T(4,128)S(1)}, f32[4,256]{1,0:T(4,128)}, u32[]{:S(2)}) copy-start(f32[4,256]{1,0:T(4,128)} %param.8) | copy-start | bytes 12292
  32.8 13.0 %collective-permute-start.3 = (f32[384,128]{1,0:T(8,128)S(1)}, f32[384,128]{1,0:T(8,128)S(1)}, u32[]{:S(2)}, u32[]{:S(2)}) collective-permute-start(f32[384,128]{1,0:T(8,128)S(1)} %bitcast.21), channel_id=1, source_target_pairs={{0,1},{1,0},{2,3},{3,2},{4,5},{5,4},{6,7},{7,6},{8,9},{9,8},{10,11... | collective-permute-start | bytes 589832 | tf_op jit(solution)/shard_map/ppermute | solution.py:19
  37.9 4.8 %collective-permute-start.5 = (f32[24,128]{1,0:T(8,128)S(1)}, f32[24,128]{1,0:T(8,128)S(1)}, u32[]{:S(2)}, u32[]{:S(2)}) collective-permute-start(f32[24,128]{1,0:T(8,128)S(1)} %get-tuple-element.5), channel_id=1, source_target_pairs={{0,128},{1,129},{2,130},{3,131},{4,132},{5,133},{6,134},{7,135},{8... | collective-permute-start | bytes 36872 | tf_op jit(solution)/shard_map/ppermute | solution.py:26
  42.6 9.9 %collective-permute-start.6 = (f32[24,128]{1,0:T(8,128)S(1)}, f32[24,128]{1,0:T(8,128)S(1)}, u32[]{:S(2)}, u32[]{:S(2)}) collective-permute-start(f32[24,128]{1,0:T(8,128)S(1)} %add.51), channel_id=1, source_target_pairs={{0,64},{1,65},{2,66},{3,67},{4,68},{5,69},{6,70},{7,71},{8,72},{9,... | collective-permute-start | bytes 36872 | tf_op jit(solution)/shard_map/ppermute | solution.py:26
  45.9 2.5 %copy-start.1 = (f32[4,5,256,256]{3,2,1,0:T(8,128)S(1)}, f32[4,5,256,256]{3,2,1,0:T(8,128)}, u32[]{:S(2)}) copy-start(f32[4,5,256,256]{3,2,1,0:T(8,128)} %rates.3) | copy-start | bytes 15728644
  51.3 2.1 %collective-permute-start.4 = (f32[24,128]{1,0:T(8,128)S(1)}, f32[24,128]{1,0:T(8,128)S(1)}, u32[]{:S(2)}, u32[]{:S(2)}) collective-permute-start(f32[24,128]{1,0:T(8,128)S(1)} %dynamic-slice_bitcast_fusion.1), channel_id=1, source_target_pairs={{0,1},{1,0},{2,3},{3,2},{4,5},{5,4},{6,7},{7,6},{8,9},{9,8},{10,11... | collective-permute-start | bytes 36872 | tf_op jit(solution)/shard_map/ppermute | solution.py:19
  53.4 4.3 %collective-permute-start.7 = (f32[24,128]{1,0:T(8,128)S(1)}, f32[24,128]{1,0:T(8,128)S(1)}, u32[]{:S(2)}, u32[]{:S(2)}) collective-permute-start(f32[24,128]{1,0:T(8,128)S(1)} %fusion.1), channel_id=1, source_target_pairs={{0,2},{1,3},{2,0},{3,1},{4,6},{5,7},{6,4},{7,5},{8,10},{9,11},{10,... | collective-permute-start | bytes 36872 | tf_op jit(solution)/shard_map/ppermute | solution.py:19
  57.7 2.1 %collective-permute-start.8 = (f32[24,128]{1,0:T(8,128)S(1)}, f32[24,128]{1,0:T(8,128)S(1)}, u32[]{:S(2)}, u32[]{:S(2)}) collective-permute-start(f32[24,128]{1,0:T(8,128)S(1)} %add.54), channel_id=1, source_target_pairs={{0,1},{1,0},{2,3},{3,2},{4,5},{5,4},{6,7},{7,6},{8,9},{9,8},{10,11... | collective-permute-start | bytes 36872 | tf_op jit(solution)/shard_map/ppermute | solution.py:19

commit v2 on v1

v2 whole, which is shorter than its diff:
```python
import jax
import jax.numpy as jnp
from jax import lax
from jax.experimental import pallas as pl
from jax.experimental.pallas import tpu as pltpu
from jax.sharding import PartitionSpec as P

Y_LO, X_HIGH, Y_HI, CORE = 128, 64, 2, 1
QUARTER_BITS = Y_LO + X_HIGH
DEVICES = 256
BLOCKS, SLOTS, COMPONENTS, STATES, HALF = 4, 5, 6, 256, 128
PAIRS = BLOCKS * SLOTS
PHONON = 64
FIRST_PHONON = 192
ROWS = BLOCKS * COMPONENTS
OWNERS = PHONON // BLOCKS
QUARTERS = [[quarter * OWNERS + owner for owner in range(OWNERS)] for quarter in range(4)]


def swap(value, bit):
    return lax.ppermute(value, ("grp", "rep"), [(i, i ^ bit) for i in range(DEVICES)])


def from_phonon(value, bits):
    pairs = [(i, i ^ bits) for i in range(DEVICES) if i & QUARTER_BITS == QUARTER_BITS]
    return lax.ppermute(value, ("grp", "rep"), pairs)


def to_phonon(value, bits):
    pairs = [(i ^ bits, i) for i in range(DEVICES) if i & QUARTER_BITS == QUARTER_BITS]
    return lax.ppermute(value, ("grp", "rep"), pairs)


def split(value):
    high = value.astype(jnp.bfloat16)
    low = (value - high.astype(jnp.float32)).astype(jnp.bfloat16)
    return high, low


def stack_split(value):
    padded = jnp.concatenate([value, jnp.zeros((2, value.shape[1]), jnp.float32)], axis=0)
    high, low = split(padded)
    both = jnp.concatenate([high.astype(jnp.float32), low.astype(jnp.float32)], axis=0)
    return high, both.astype(jnp.bfloat16)


def product(high, both, weights, contract):
    rates_high, rates_low = split(weights)
    dims = (((1,), (contract,)), ((), ()))
    main = lax.dot_general(both, rates_high, dims, preferred_element_type=jnp.float32)
    rest = lax.dot_general(high, rates_low, dims, preferred_element_type=jnp.float32)
    return main[:8] + main[8:] + rest


def rate_copies(count_hbm, partner_hbm, rates, count, partner, held, sems, small_sems):
    def fetch(block, slot):
        pair = block * SLOTS + slot
        return pltpu.make_async_copy(rates.at[block, slot], held.at[pair], sems.at[pair])

    counts = pltpu.make_async_copy(count_hbm, count, small_sems.at[0])
    partners = pltpu.make_async_copy(partner_hbm, partner, small_sems.at[1])
    counts.start()
    partners.start()
    for block in range(BLOCKS):
        fetch(block, 0).start()
    counts.wait()
    for block in range(BLOCKS):

        @pl.loop(1, count[0, block])
        def _(slot):
            fetch(block, slot).start()

    partners.wait()
    return fetch


def spread_kernel(
    count_hbm, partner_hbm, deviation, rates, keep, give, own, held, count, partner, own_sem, sems, small
):
    keep[...] = jnp.zeros_like(keep)
    give[...] = jnp.zeros_like(give)
    is_electron = lax.axis_index("grp") < 3 * OWNERS
    core = lax.rem(lax.axis_index("rep"), 2)

    @pl.when(is_electron)
    def _():
        own_copy = pltpu.make_async_copy(deviation, own, own_sem)
        own_copy.start()
        fetch = rate_copies(count_hbm, partner_hbm, rates, count, partner, held, sems, small)
        own_copy.wait()
        for block in range(BLOCKS):
            rows = [own[component, block : block + 1, :] for component in range(COMPONENTS)]
            high, both = stack_split(jnp.concatenate(rows, axis=0))

            @pl.loop(0, count[0, block])
            def _(slot):
                fetch(block, slot).wait()
                value = product(high, both, held[block * SLOTS + slot], 0)[:COMPONENTS]
                left, right = value[:, :HALF], value[:, HALF:]
                row = (partner[block, slot] - FIRST_PHONON) * COMPONENTS
                keep[pl.ds(row, COMPONENTS), :] += jnp.where(core == 0, left, right)
                give[pl.ds(row, COMPONENTS), :] += jnp.where(core == 0, right, left)


def forward_kernel(
    count_hbm, partner_hbm, mine, other, rates, keep, give, held, count, partner, sems, small
):
    core = lax.rem(lax.axis_index("rep"), 2)
    fetch = rate_copies(count_hbm, partner_hbm, rates, count, partner, held, sems, small)
    for block in range(BLOCKS):

        def visit(slot, total):
            fetch(block, slot).wait()
            row = (partner[block, slot] - FIRST_PHONON) * COMPONENTS
            near, far = mine[pl.ds(row, COMPONENTS), :], other[pl.ds(row, COMPONENTS), :]
            left, right = jnp.where(core == 0, near, far), jnp.where(core == 0, far, near)
            high, both = stack_split(jnp.concatenate([left, right], axis=1))
            return total + product(high, both, held[block * SLOTS + slot], 1)

        total = lax.fori_loop(0, count[0, block], visit, jnp.zeros((8, STATES), jnp.float32))
        left, right = total[:COMPONENTS, :HALF], total[:COMPONENTS, HALF:]
        rows = slice(block * COMPONENTS, (block + 1) * COMPONENTS)
        keep[rows, :] = jnp.where(core == 0, left, right)
        give[rows, :] = jnp.where(core == 0, right, left)


VMEM = pl.BlockSpec(memory_space=pltpu.VMEM)
HBM = pl.BlockSpec(memory_space=pltpu.HBM)
RATE_SCRATCH = [
    pltpu.VMEM((PAIRS, STATES, STATES), jnp.float32),
    pltpu.SMEM((1, BLOCKS), jnp.int32),
    pltpu.SMEM((BLOCKS, SLOTS), jnp.int32),
]
RATE_SEMS = [pltpu.SemaphoreType.DMA((PAIRS,)), pltpu.SemaphoreType.DMA((2,))]


def rate_kernel(body, name, rows, in_specs, first_scratch, later_sems):
    return pl.pallas_call(
        body,
        name=name,
        out_shape=[jax.ShapeDtypeStruct((rows, HALF), jnp.float32)] * 2,
        in_specs=in_specs,
        out_specs=[VMEM] * 2,
        scratch_shapes=first_scratch + RATE_SCRATCH + later_sems + RATE_SEMS,
        compiler_params=pltpu.CompilerParams(vmem_limit_bytes=16 * 1024 * 1024),
        cost_estimate=pl.CostEstimate(
            flops=6 * PAIRS * 8 * STATES * STATES,
            bytes_accessed=2 * PAIRS * STATES * STATES * 4,
            transcendentals=0,
        ),
    )


def in_hbm(*values):
    return [pltpu.with_memory_space_constraint(value, pltpu.HBM) for value in values]


def spread(count, partner, deviation, rates):
    own = pltpu.VMEM((COMPONENTS, BLOCKS, STATES), jnp.float32)
    return rate_kernel(
        spread_kernel, "spread", PHONON * COMPONENTS, [HBM] * 4, [own], [pltpu.SemaphoreType.DMA]
    )(*in_hbm(count, partner, deviation, rates))


def forward(count, partner, mine, other, rates):
    count, partner, rates = in_hbm(count, partner, rates)
    return rate_kernel(forward_kernel, "forward", ROWS, [HBM, HBM, VMEM, VMEM, HBM], [], [])(
        count, partner, mine, other, rates
    )


def on_device(deviation, source, lifetime, rates, partner, count):
    core = lax.axis_index("rep") % 2
    is_phonon = lax.axis_index("grp") >= 3 * OWNERS
    live = count.T
    turned = deviation.transpose(1, 0, 2)

    def both_halves(mine, other):
        left, right = jnp.where(core == 0, mine, other), jnp.where(core == 0, other, mine)
        return jnp.concatenate([left, right], axis=-1)

    arrived = [swap(turned, bits) for bits in (QUARTER_BITS, X_HIGH, Y_LO)]
    quarter = lax.axis_index("grp") // OWNERS
    carried = jnp.where(quarter == 0, arrived[0], jnp.where(quarter == 1, arrived[2], arrived[1]))
    carried = jnp.where(is_phonon, turned, carried)
    carried = lax.dynamic_slice_in_dim(carried, core * HALF, HALF, 2)
    carried = carried.transpose(1, 0, 2).reshape(ROWS, HALF)

    keep, give = spread(live, partner, turned, rates)
    drag = keep + swap(give, CORE)

    parcel = jnp.concatenate(
        [drag.reshape(OWNERS, ROWS, HALF), jnp.broadcast_to(carried, (OWNERS, ROWS, HALF))], axis=1
    )
    arrived = lax.all_to_all(parcel, "grp", 0, 0, axis_index_groups=QUARTERS, tiled=True)
    drag = arrived[:, :ROWS].sum(0)
    phonon = arrived[:, ROWS:].reshape(PHONON * COMPONENTS, HALF)

    others = [swap(drag, bits) for bits in (QUARTER_BITS, X_HIGH, Y_LO)]
    keep, give = forward(live, partner, phonon, swap(phonon, CORE), rates)
    total = keep + swap(give, CORE)
    total = total + jnp.where(is_phonon, drag + others[0] + others[1] + others[2], 0.0)
    total = total + swap(total, Y_HI)
    summed = both_halves(total, swap(total, CORE)).reshape(BLOCKS, COMPONENTS, STATES)
    return source + lifetime[:, None, :] * summed


def solution(mesh):
    placed = (
        P("grp", None, None),
        P("grp", None, None),
        P("grp", None),
        P("grp", "rep", None, None),
        P("grp", "rep"),
        P("grp", "rep"),
    )
    return jax.shard_map(
        on_device, mesh=mesh, in_specs=placed, out_specs=P("grp", None, None), check_vma=False
    )
```

time: 60.8 us -> 51.8 us (0.85)
  local copies, waits for them, and re-layouts: 7.2 us -> 0.66 us
  starting transfers between devices: 23.2 us -> 18.7 us
  Pallas kernels: 5.48 us -> 7.57 us
  other arithmetic: 1.56 us -> 0.13 us
  blocking collectives: 18.1 us -> 19.4 us
    ppermute x4 -> x0, starting transfers between devices: 9.05 us -> none  [push(): return lax.ppermute(value, ('grp', 'rep'), pairs)]
    unnamed x11 -> x6, local copies, waits for them, and re-layouts: 5.72 us -> 0.02 us
    ppermute x5 -> x11, starting transfers between devices: 14.1 us -> 18.7 us  [swap(): lax.ppermute(value, ('grp', 'rep'), [(i, i ^ bit) for i in range(DEVICES)])]
    ppermute x5 -> x11, waiting for transfers between devices: 2.75 us -> 5.04 us  [swap(): lax.ppermute(value, ('grp', 'rep'), [(i, i ^ bit) for i in range(DEVICES)])]
    ppermute x4 -> x0, waiting for transfers between devices: 2.1 us -> none  [push(): return lax.ppermute(value, ('grp', 'rep'), pairs)]
    pallas_call x2, Pallas kernels: 5.48 us -> 7.57 us  [the longest x1 3.94 us: forward(): rate_kernel(forward_kernel, 'forward', ROWS, [HBM, HBM, VMEM, VMEM, HBM],...]
    all_to_all x1, blocking collectives: 18.1 us -> 19.4 us  [on_device(): lax.all_to_all(parcel, 'grp', 0, 0, axis_index_groups=QUARTERS, tiled=True)]
    dynamic_slice x2 -> x0, local copies, waits for them, and re-layouts: 0.71 us -> none  [on_device(): lax.dynamic_slice_in_dim(deviation, core * HALF, HALF, 2)]
  transfers between devices with their start and end apart: 9 -> 11, of which waited for: 5 -> 4; matrix products, arithmetic and copies ran while one was open for 4% -> 0% of each run, Pallas kernels for 9% -> 8%
where the time goes in v2:
time: 51.8 us; the launch traced here: 51.7 us
  blocking collectives  19.4 us (37%)
  starting transfers between devices  18.7 us (36%)
  Pallas kernels  7.57 us (15%)
  waiting for transfers between devices  5.04 us (10%)
  local copies, waits for them, and re-layouts  0.66 us (1%)
    all_to_all x1, blocking collectives, on_device(): lax.all_to_all(parcel, 'grp', 0, 0, axis_index_groups=QUARTERS, tiled=True)  19.4 us
    ppermute x11, starting transfers between devices, swap(): lax.ppermute(value, ('grp', 'rep'), [(i, i ^ bit) for i in range(DEVICES)])  18.7 us
    ppermute x11, waiting for transfers between devices, swap(): lax.ppermute(value, ('grp', 'rep'), [(i, i ^ bit) for i in range(DEVICES)])  5.04 us
    pallas_call x1, Pallas kernels, forward(): rate_kernel(forward_kernel, 'forward', ROWS, [HBM, HBM, VMEM, VMEM, HBM],...  3.94 us
    pallas_call x1, Pallas kernels, spread(): rate_kernel(spread_kernel, 'spread', PHONON * COMPONENTS, [HBM] * 4, [own...  3.63 us
  transfers between devices with their start and end apart: 11, of which 4 were waited for; matrix products, arithmetic and copies ran while one was open for 0% of the time, Pallas kernels for 8%

profile of v2, /device:TPU:1, one launch (start us, length us, event | category | flops | bytes accessed | tf_op | source)
XLA Modules:
  0.0 51.7 jit_solution(17846271444359839232)
XLA Ops:
  0.0 0.0 copy-start
  0.0 3.6 %spread.1 = (f32[384,128]{1,0:T(8,128)S(1)}, f32[384,128]{1,0:T(8,128)S(1)}) custom-call(s32[1,4]{1,0:T(1,128)} %bitcast.14, s32[4,5]{1,0:T(4,128)} %partner_hbm.3, f32[6,4,256]{2,1,0:T(4,128)} %bitcast.9, f32[4,5,256,256]{3,2,1,0:T(8,128)} %rates.3), custom_call_target="tpu_custom_call" | custom-call | flops 62914560 | bytes 10485760 | tf_op jit(solution)/shard_map/spread/pallas_call | solution.py:160
  3.6 0.0 copy-start.1
  3.7 0.0 copy-start.2
  3.7 2.4 %collective-permute-start = (f32[384,128]{1,0:T(8,128)S(1)}, f32[384,128]{1,0:T(8,128)S(1)}, u32[]{:S(2)}, u32[]{:S(2)}) collective-permute-start(f32[384,128]{1,0:T(8,128)S(1)} %get-tuple-element.10), channel_id=1, source_target_pairs={{0,1},{1,0},{2,3},{3,2},{4,5},{5,4},{6,7},{7,6},{8,9},{9,8},{10,11... | collective-permute-start | bytes 589832 | tf_op jit(solution)/shard_map/ppermute | solution.py:21
  6.1 0.0 copy-done
  6.1 0.9 %collective-permute-start.3 = (f32[6,4,256]{2,1,0:T(4,128)S(1)}, f32[6,4,256]{2,1,0:T(4,128)S(1)}, u32[]{:S(2)}, u32[]{:S(2)}) collective-permute-start(f32[6,4,256]{2,1,0:T(4,128)S(1)} %bitcast.10), channel_id=1, source_target_pairs={{0,64},{1,65},{2,66},{3,67},{4,68},{5,69},{6,70},{7,71},{8,72},{9,... | collective-permute-start | bytes 73736 | tf_op jit(solution)/shard_map/ppermute | solution.py:21
  7.0 0.0 collective-permute-start.2
  7.0 3.3 %collective-permute-start.1 = (f32[6,4,256]{2,1,0:T(4,128)S(1)}, f32[6,4,256]{2,1,0:T(4,128)S(1)}, u32[]{:S(2)}, u32[]{:S(2)}) collective-permute-start(f32[6,4,256]{2,1,0:T(4,128)S(1)} %bitcast.12), channel_id=1, source_target_pairs={{0,192},{1,193},{2,194},{3,195},{4,196},{5,197},{6,198},{7,199},{8... | collective-permute-start | bytes 73736 | tf_op jit(solution)/shard_map/ppermute | solution.py:21
  10.2 0.0 collective-permute-done.3
  10.3 0.0 collective-permute-done.2
  10.3 1.8 %collective-permute-done.1 = f32[6,4,256]{2,1,0:T(4,128)S(1)} collective-permute-done((f32[6,4,256]{2,1,0:T(4,128)S(1)}, f32[6,4,256]{2,1,0:T(4,128)S(1)}, u32[]{:S(2)}, u32[]{:S(2)}) %collective-permute-start.1) | collective-permute-done | bytes 24608 | tf_op jit(solution)/shard_map/ppermute | solution.py:21
  12.1 0.0 collective-permute-done
  12.2 19.4 %all_to_all.5 = f32[16,48,128]{2,1,0:T(8,128)S(1)} all-to-all(f32[16,48,128]{2,1,0:T(8,128)S(1)} %pad_maximum_fusion), channel_id=1, replica_groups={{0,4,8,12,16,20,24,28,32,36,40,44,48,52,56,60},{64,68,72,76,80,84,88,92..., dimensions={0} | all-to-all | bytes 786432 | tf_op jit(solution)/shard_map/all_to_all | solution.py:195
  31.7 2.9 %collective-permute-start.4 = (f32[384,128]{1,0:T(8,128)S(1)}, f32[384,128]{1,0:T(8,128)S(1)}, u32[]{:S(2)}, u32[]{:S(2)}) collective-permute-start(f32[384,128]{1,0:T(8,128)S(1)} %bitcast.6), channel_id=1, source_target_pairs={{0,1},{1,0},{2,3},{3,2},{4,5},{5,4},{6,7},{7,6},{8,9},{9,8},{10,11... | collective-permute-start | bytes 589832 | tf_op jit(solution)/shard_map/ppermute | solution.py:21
  34.6 1.4 %collective-permute-start.8 = (f32[24,128]{1,0:T(8,128)S(1)}, f32[24,128]{1,0:T(8,128)S(1)}, u32[]{:S(2)}, u32[]{:S(2)}) collective-permute-start(f32[24,128]{1,0:T(8,128)S(1)} %get-tuple-element.14), channel_id=1, source_target_pairs={{0,128},{1,129},{2,130},{3,131},{4,132},{5,133},{6,134},{7,135},{8... | collective-permute-start | bytes 36872 | tf_op jit(solution)/shard_map/ppermute | solution.py:21
  36.0 2.1 %collective-permute-start.7 = (f32[24,128]{1,0:T(8,128)S(1)}, f32[24,128]{1,0:T(8,128)S(1)}, u32[]{:S(2)}, u32[]{:S(2)}) collective-permute-start(f32[24,128]{1,0:T(8,128)S(1)} %get-tuple-element.14), channel_id=1, source_target_pairs={{0,64},{1,65},{2,66},{3,67},{4,68},{5,69},{6,70},{7,71},{8,72},{9,... | collective-permute-start | bytes 36872 | tf_op jit(solution)/shard_map/ppermute | solution.py:21
  38.1 1.1 %collective-permute-start.6 = (f32[24,128]{1,0:T(8,128)S(1)}, f32[24,128]{1,0:T(8,128)S(1)}, u32[]{:S(2)}, u32[]{:S(2)}) collective-permute-start(f32[24,128]{1,0:T(8,128)S(1)} %get-tuple-element.14), channel_id=1, source_target_pairs={{0,192},{1,193},{2,194},{3,195},{4,196},{5,197},{6,198},{7,199},{8... | collective-permute-start | bytes 36872 | tf_op jit(solution)/shard_map/ppermute | solution.py:21
  39.2 0.0 collective-permute-done.4.other
  39.2 3.9 %forward.1 = (f32[24,128]{1,0:T(8,128)S(1)}, f32[24,128]{1,0:T(8,128)S(1)}) custom-call(s32[1,4]{1,0:T(1,128)} %bitcast.15, s32[4,5]{1,0:T(4,128)} %partner_hbm.3, f32[384,128]{1,0:T(8,128)S(1)} %bitcast.7, f32[384,128]{1,0:T(8,128)S(1)} %collective-permute-done.4.other, f32[4,5,256,256]{3,2,1,0:T(8,128)} %rates.3), custom_call_target="tpu_custom_call" | custom-call | flops 62914560 | bytes 10485760 | tf_op jit(solution)/shard_map/forward/pallas_call | solution.py:167
  43.1 0.1 collective-permute-start.5
  43.2 0.0 collective-permute-done.8
  43.3 0.0 collective-permute-done.7
  43.3 0.0 collective-permute-done.6
  43.3 1.1 %collective-permute-done.5 = f32[24,128]{1,0:T(8,128)S(1)} collective-permute-done((f32[24,128]{1,0:T(8,128)S(1)}, f32[24,128]{1,0:T(8,128)S(1)}, u32[]{:S(2)}, u32[]{:S(2)}) %collective-permute-start.5) | collective-permute-done | bytes 12320 | tf_op jit(solution)/shard_map/ppermute | solution.py:21
  44.4 2.9 %collective-permute-start.9 = (f32[24,128]{1,0:T(8,128)S(1)}, f32[24,128]{1,0:T(8,128)S(1)}, u32[]{:S(2)}, u32[]{:S(2)}) collective-permute-start(f32[24,128]{1,0:T(8,128)S(1)} %select_add_fusion), channel_id=1, source_target_pairs={{0,2},{1,3},{2,0},{3,1},{4,6},{5,7},{6,4},{7,5},{8,10},{9,11},{10,... | collective-permute-start | bytes 36872 | tf_op jit(solution)/shard_map/ppermute | solution.py:21
  47.3 1.2 %collective-permute-done.9 = f32[24,128]{1,0:T(8,128)S(1)} collective-permute-done((f32[24,128]{1,0:T(8,128)S(1)}, f32[24,128]{1,0:T(8,128)S(1)}, u32[]{:S(2)}, u32[]{:S(2)}) %collective-permute-start.9) | collective-permute-done | bytes 12320 | tf_op jit(solution)/shard_map/ppermute | solution.py:21
  48.6 1.6 %collective-permute-start.10 = (f32[24,128]{1,0:T(8,128)S(1)}, f32[24,128]{1,0:T(8,128)S(1)}, u32[]{:S(2)}, u32[]{:S(2)}) collective-permute-start(f32[24,128]{1,0:T(8,128)S(1)} %add.40), channel_id=1, source_target_pairs={{0,1},{1,0},{2,3},{3,2},{4,5},{5,4},{6,7},{7,6},{8,9},{9,8},{10,11... | collective-permute-start | bytes 36872 | tf_op jit(solution)/shard_map/ppermute | solution.py:21
  50.2 0.8 %collective-permute-done.10 = f32[24,128]{1,0:T(8,128)S(1)} collective-permute-done((f32[24,128]{1,0:T(8,128)S(1)}, f32[24,128]{1,0:T(8,128)S(1)}, u32[]{:S(2)}, u32[]{:S(2)}) %collective-permute-start.10) | collective-permute-done | bytes 12320 | tf_op jit(solution)/shard_map/ppermute | solution.py:21
  51.0 0.0 copy-done.1
  51.0 0.0 copy-done.2
  51.1 0.6 %copy.10 = f32[4,6,256]{2,0,1:T(4,128)} copy(f32[4,6,256]{2,1,0:T(8,128)S(1)} %copy_add_fusion) | data formatting | bytes 49152 | tf_op jit(solution)/shard_map/add | solution.py:205
  (13 shorter events, 0.2 us)
Async XLA Ops:
  0.0 6.1 %copy-start = (f32[4,6,256]{2,0,1:T(4,128)S(1)}, f32[4,6,256]{2,0,1:T(4,128)}, u32[]{:S(2)}) copy-start(f32[4,6,256]{2,0,1:T(4,128)} %param.6) | copy-start | bytes 73732
  3.6 47.4 %copy-start.1 = (f32[4,6,256]{2,0,1:T(4,128)S(1)}, f32[4,6,256]{2,0,1:T(4,128)}, u32[]{:S(2)}) copy-start(f32[4,6,256]{2,0,1:T(4,128)} %param.7) | copy-start | bytes 73732
  3.7 47.4 %copy-start.2 = (f32[4,256]{1,0:T(4,128)S(1)}, f32[4,256]{1,0:T(4,128)}, u32[]{:S(2)}) copy-start(f32[4,256]{1,0:T(4,128)} %param.8) | copy-start | bytes 12292
  3.7 8.4 %collective-permute-start = (f32[384,128]{1,0:T(8,128)S(1)}, f32[384,128]{1,0:T(8,128)S(1)}, u32[]{:S(2)}, u32[]{:S(2)}) collective-permute-start(f32[384,128]{1,0:T(8,128)S(1)} %get-tuple-element.10), channel_id=1, source_target_pairs={{0,1},{1,0},{2,3},{3,2},{4,5},{5,4},{6,7},{7,6},{8,9},{9,8},{10,11... | collective-permute-start | bytes 589832 | tf_op jit(solution)/shard_map/ppermute | solution.py:21
  6.1 4.2 %collective-permute-start.3 = (f32[6,4,256]{2,1,0:T(4,128)S(1)}, f32[6,4,256]{2,1,0:T(4,128)S(1)}, u32[]{:S(2)}, u32[]{:S(2)}) collective-permute-start(f32[6,4,256]{2,1,0:T(4,128)S(1)} %bitcast.10), channel_id=1, source_target_pairs={{0,64},{1,65},{2,66},{3,67},{4,68},{5,69},{6,70},{7,71},{8,72},{9,... | collective-permute-start | bytes 73736 | tf_op jit(solution)/shard_map/ppermute | solution.py:21
  7.0 3.3 %collective-permute-start.2 = (f32[6,4,256]{2,1,0:T(4,128)S(1)}, f32[6,4,256]{2,1,0:T(4,128)S(1)}, u32[]{:S(2)}, u32[]{:S(2)}) collective-permute-start(f32[6,4,256]{2,1,0:T(4,128)S(1)} %bitcast.11), channel_id=1, source_target_pairs={{0,128},{1,129},{2,130},{3,131},{4,132},{5,133},{6,134},{7,135},{8... | collective-permute-start | bytes 73736 | tf_op jit(solution)/shard_map/ppermute | solution.py:21
  7.0 5.1 %collective-permute-start.1 = (f32[6,4,256]{2,1,0:T(4,128)S(1)}, f32[6,4,256]{2,1,0:T(4,128)S(1)}, u32[]{:S(2)}, u32[]{:S(2)}) collective-permute-start(f32[6,4,256]{2,1,0:T(4,128)S(1)} %bitcast.12), channel_id=1, source_target_pairs={{0,192},{1,193},{2,194},{3,195},{4,196},{5,197},{6,198},{7,199},{8... | collective-permute-start | bytes 73736 | tf_op jit(solution)/shard_map/ppermute | solution.py:21
  31.7 7.5 %collective-permute-start.4 = (f32[384,128]{1,0:T(8,128)S(1)}, f32[384,128]{1,0:T(8,128)S(1)}, u32[]{:S(2)}, u32[]{:S(2)}) collective-permute-start(f32[384,128]{1,0:T(8,128)S(1)} %bitcast.6), channel_id=1, source_target_pairs={{0,1},{1,0},{2,3},{3,2},{4,5},{5,4},{6,7},{7,6},{8,9},{9,8},{10,11... | collective-permute-start | bytes 589832 | tf_op jit(solution)/shard_map/ppermute | solution.py:21
  34.6 8.6 %collective-permute-start.8 = (f32[24,128]{1,0:T(8,128)S(1)}, f32[24,128]{1,0:T(8,128)S(1)}, u32[]{:S(2)}, u32[]{:S(2)}) collective-permute-start(f32[24,128]{1,0:T(8,128)S(1)} %get-tuple-element.14), channel_id=1, source_target_pairs={{0,128},{1,129},{2,130},{3,131},{4,132},{5,133},{6,134},{7,135},{8... | collective-permute-start | bytes 36872 | tf_op jit(solution)/shard_map/ppermute | solution.py:21
  36.0 7.3 %collective-permute-start.7 = (f32[24,128]{1,0:T(8,128)S(1)}, f32[24,128]{1,0:T(8,128)S(1)}, u32[]{:S(2)}, u32[]{:S(2)}) collective-permute-start(f32[24,128]{1,0:T(8,128)S(1)} %get-tuple-element.14), channel_id=1, source_target_pairs={{0,64},{1,65},{2,66},{3,67},{4,68},{5,69},{6,70},{7,71},{8,72},{9,... | collective-permute-start | bytes 36872 | tf_op jit(solution)/shard_map/ppermute | solution.py:21
  38.1 5.1 %collective-permute-start.6 = (f32[24,128]{1,0:T(8,128)S(1)}, f32[24,128]{1,0:T(8,128)S(1)}, u32[]{:S(2)}, u32[]{:S(2)}) collective-permute-start(f32[24,128]{1,0:T(8,128)S(1)} %get-tuple-element.14), channel_id=1, source_target_pairs={{0,192},{1,193},{2,194},{3,195},{4,196},{5,197},{6,198},{7,199},{8... | collective-permute-start | bytes 36872 | tf_op jit(solution)/shard_map/ppermute | solution.py:21
  43.1 1.3 %collective-permute-start.5 = (f32[24,128]{1,0:T(8,128)S(1)}, f32[24,128]{1,0:T(8,128)S(1)}, u32[]{:S(2)}, u32[]{:S(2)}) collective-permute-start(f32[24,128]{1,0:T(8,128)S(1)} %get-tuple-element.12), channel_id=1, source_target_pairs={{0,1},{1,0},{2,3},{3,2},{4,5},{5,4},{6,7},{7,6},{8,9},{9,8},{10,11... | collective-permute-start | bytes 36872 | tf_op jit(solution)/shard_map/ppermute | solution.py:21
  44.4 4.1 %collective-permute-start.9 = (f32[24,128]{1,0:T(8,128)S(1)}, f32[24,128]{1,0:T(8,128)S(1)}, u32[]{:S(2)}, u32[]{:S(2)}) collective-permute-start(f32[24,128]{1,0:T(8,128)S(1)} %select_add_fusion), channel_id=1, source_target_pairs={{0,2},{1,3},{2,0},{3,1},{4,6},{5,7},{6,4},{7,5},{8,10},{9,11},{10,... | collective-permute-start | bytes 36872 | tf_op jit(solution)/shard_map/ppermute | solution.py:21
  48.6 2.4 %collective-permute-start.10 = (f32[24,128]{1,0:T(8,128)S(1)}, f32[24,128]{1,0:T(8,128)S(1)}, u32[]{:S(2)}, u32[]{:S(2)}) collective-permute-start(f32[24,128]{1,0:T(8,128)S(1)} %add.40), channel_id=1, source_target_pairs={{0,1},{1,0},{2,3},{3,2},{4,5},{5,4},{6,7},{7,6},{8,9},{9,8},{10,11... | collective-permute-start | bytes 36872 | tf_op jit(solution)/shard_map/ppermute | solution.py:21

commit v3 on v2

--- a/solution.py
+++ b/solution.py
@@ -10,6 +10,7 @@
 DEVICES = 256
 BLOCKS, SLOTS, COMPONENTS, STATES, HALF = 4, 5, 6, 256, 128
 PAIRS = BLOCKS * SLOTS
+UNROLL = 4
 PHONON = 64
 FIRST_PHONON = 192
 ROWS = BLOCKS * COMPONENTS
@@ -38,8 +39,7 @@
 
 
 def stack_split(value):
-    padded = jnp.concatenate([value, jnp.zeros((2, value.shape[1]), jnp.float32)], axis=0)
-    high, low = split(padded)
+    high, low = split(value)
     both = jnp.concatenate([high.astype(jnp.float32), low.astype(jnp.float32)], axis=0)
     return high, both.astype(jnp.bfloat16)
 
@@ -74,51 +74,85 @@
     return fetch
 
 
+def visit_live(count, chosen, fetch, visit):
+    total = jnp.int32(0)
+    for block in range(BLOCKS):
+
+        def note(slot, at):
+            chosen[at] = block * SLOTS + slot
+            return at + 1
+
+        total = lax.fori_loop(0, count[0, block], note, total)
+
+    @pl.loop(0, lax.div(total + (UNROLL - 1), UNROLL))
+    def _(step):
+        places = [step * UNROLL + offset for offset in range(UNROLL)]
+        pairs = [chosen[jnp.minimum(place, total - 1)] for place in places]
+        blocks = [lax.div(pair, SLOTS) for pair in pairs]
+        slots = [pair - SLOTS * block for pair, block in zip(pairs, blocks)]
+        for place, block, slot in zip(places, blocks, slots):
+
+            @pl.when(place < total)
+            def _():
+                fetch(block, slot).wait()
+
+        visit([(block, slot, place < total) for block, slot, place in zip(blocks, slots, places)])
+
+
 def spread_kernel(
-    count_hbm, partner_hbm, deviation, rates, keep, give, own, held, count, partner, own_sem, sems, small
+    count_hbm, partner_hbm, deviation, rates, keep, give, own, rows, held, count, partner, chosen, own_sem, sems, small
 ):
     keep[...] = jnp.zeros_like(keep)
     give[...] = jnp.zeros_like(give)
-    is_electron = lax.axis_index("grp") < 3 * OWNERS
     core = lax.rem(lax.axis_index("rep"), 2)
 
-    @pl.when(is_electron)
+    @pl.when(lax.axis_index("grp") < 3 * OWNERS)
     def _():
         own_copy = pltpu.make_async_copy(deviation, own, own_sem)
         own_copy.start()
         fetch = rate_copies(count_hbm, partner_hbm, rates, count, partner, held, sems, small)
         own_copy.wait()
         for block in range(BLOCKS):
-            rows = [own[component, block : block + 1, :] for component in range(COMPONENTS)]
-            high, both = stack_split(jnp.concatenate(rows, axis=0))
-
-            @pl.loop(0, count[0, block])
-            def _(slot):
-                fetch(block, slot).wait()
-                value = product(high, both, held[block * SLOTS + slot], 0)[:COMPONENTS]
+            parts = [own[component, block : block + 1, :] for component in range(COMPONENTS)]
+            rows[block] = jnp.concatenate(parts + [jnp.zeros((2, STATES), jnp.float32)], axis=0)
+
+        def visit(some):
+            values = []
+            for block, slot, live in some:
+                high, both = stack_split(jnp.where(live, rows[block], 0.0))
+                values.append(product(high, both, held[block * SLOTS + slot], 0)[:COMPONENTS])
+            for (block, slot, live), value in zip(some, values):
                 left, right = value[:, :HALF], value[:, HALF:]
                 row = (partner[block, slot] - FIRST_PHONON) * COMPONENTS
                 keep[pl.ds(row, COMPONENTS), :] += jnp.where(core == 0, left, right)
                 give[pl.ds(row, COMPONENTS), :] += jnp.where(core == 0, right, left)
 
+        visit_live(count, chosen, fetch, visit)
+
 
 def forward_kernel(
-    count_hbm, partner_hbm, mine, other, rates, keep, give, held, count, partner, sems, small
+    count_hbm, partner_hbm, mine, other, rates, keep, give, totals, held, count, partner, chosen, sems, small
 ):
     core = lax.rem(lax.axis_index("rep"), 2)
     fetch = rate_copies(count_hbm, partner_hbm, rates, count, partner, held, sems, small)
-    for block in range(BLOCKS):
-
-        def visit(slot, total):
-            fetch(block, slot).wait()
+    totals[...] = jnp.zeros_like(totals)
+
+    def visit(some):
+        values = []
+        for block, slot, live in some:
             row = (partner[block, slot] - FIRST_PHONON) * COMPONENTS
             near, far = mine[pl.ds(row, COMPONENTS), :], other[pl.ds(row, COMPONENTS), :]
             left, right = jnp.where(core == 0, near, far), jnp.where(core == 0, far, near)
-            high, both = stack_split(jnp.concatenate([left, right], axis=1))
-            return total + product(high, both, held[block * SLOTS + slot], 1)
-
-        total = lax.fori_loop(0, count[0, block], visit, jnp.zeros((8, STATES), jnp.float32))
-        left, right = total[:COMPONENTS, :HALF], total[:COMPONENTS, HALF:]
+            picked = jnp.concatenate([left, right], axis=1)
+            padded = jnp.concatenate([picked, jnp.zeros((2, STATES), jnp.float32)], axis=0)
+            high, both = stack_split(jnp.where(live, padded, 0.0))
+            values.append(product(high, both, held[block * SLOTS + slot], 1))
+        for (block, slot, live), value in zip(some, values):
+            totals[block] += value
+
+    visit_live(count, chosen, fetch, visit)
+    for block in range(BLOCKS):
+        left, right = totals[block, :COMPONENTS, :HALF], totals[block, :COMPONENTS, HALF:]
         rows = slice(block * COMPONENTS, (block + 1) * COMPONENTS)
         keep[rows, :] = jnp.where(core == 0, left, right)
         give[rows, :] = jnp.where(core == 0, right, left)
@@ -130,17 +164,18 @@
     pltpu.VMEM((PAIRS, STATES, STATES), jnp.float32),
     pltpu.SMEM((1, BLOCKS), jnp.int32),
     pltpu.SMEM((BLOCKS, SLOTS), jnp.int32),
+    pltpu.SMEM((PAIRS,), jnp.int32),
 ]
 RATE_SEMS = [pltpu.SemaphoreType.DMA((PAIRS,)), pltpu.SemaphoreType.DMA((2,))]
 
 
-def rate_kernel(body, name, rows, in_specs, first_scratch, later_sems):
+def rate_kernel(body, name, outs, in_specs, first_scratch, later_sems):
     return pl.pallas_call(
         body,
         name=name,
-        out_shape=[jax.ShapeDtypeStruct((rows, HALF), jnp.float32)] * 2,
+        out_shape=[jax.ShapeDtypeStruct((rows, HALF), jnp.float32) for rows in outs],
         in_specs=in_specs,
-        out_specs=[VMEM] * 2,
+        out_specs=[VMEM] * len(outs),
         scratch_shapes=first_scratch + RATE_SCRATCH + later_sems + RATE_SEMS,
         compiler_params=pltpu.CompilerParams(vmem_limit_bytes=16 * 1024 * 1024),
         cost_estimate=pl.CostEstimate(
@@ -156,17 +191,20 @@
 
 
 def spread(count, partner, deviation, rates):
+    outs = [PHONON * COMPONENTS] * 2
     own = pltpu.VMEM((COMPONENTS, BLOCKS, STATES), jnp.float32)
+    padded = pltpu.VMEM((BLOCKS, 8, STATES), jnp.float32)
     return rate_kernel(
-        spread_kernel, "spread", PHONON * COMPONENTS, [HBM] * 4, [own], [pltpu.SemaphoreType.DMA]
+        spread_kernel, "spread", outs, [HBM] * 4, [own, padded], [pltpu.SemaphoreType.DMA]
     )(*in_hbm(count, partner, deviation, rates))
 
 
 def forward(count, partner, mine, other, rates):
     count, partner, rates = in_hbm(count, partner, rates)
-    return rate_kernel(forward_kernel, "forward", ROWS, [HBM, HBM, VMEM, VMEM, HBM], [], [])(
-        count, partner, mine, other, rates
-    )
+    totals = pltpu.VMEM((BLOCKS, 8, STATES), jnp.float32)
+    return rate_kernel(
+        forward_kernel, "forward", [ROWS] * 2, [HBM, HBM, VMEM, VMEM, HBM], [totals], []
+    )(count, partner, mine, other, rates)
 
 
 def on_device(deviation, source, lifetime, rates, partner, count):

time: 51.8 us -> 51.2 us (0.988)
  starting transfers between devices: 18.7 us -> 21.2 us
  Pallas kernels: 7.57 us -> 5.26 us
  waiting for transfers between devices: 5.04 us -> 4.19 us
    ppermute x11, starting transfers between devices: 18.7 us -> 21.2 us  [swap(): lax.ppermute(value, ('grp', 'rep'), [(i, i ^ bit) for i in range(DEVICES)])]
    pallas_call x2, Pallas kernels: 7.57 us -> 5.26 us  [the longest x1 2.69 us: forward(): rate_kernel(forward_kernel, 'forward', [ROWS] * 2, [HBM, HBM, VMEM, VMEM,...]
    ppermute x11, waiting for transfers between devices: 5.04 us -> 4.19 us  [swap(): lax.ppermute(value, ('grp', 'rep'), [(i, i ^ bit) for i in range(DEVICES)])]
  transfers between devices with their start and end apart: 11 -> 11, of which waited for: 4 -> 4; matrix products, arithmetic and copies ran while one was open for 0% -> 0% of each run, Pallas kernels for 8% -> 5%
where the time goes in v3:
time: 51.2 us; the launch traced here: 51 us
  starting transfers between devices  21.2 us (41%)
  blocking collectives  19.4 us (38%)
  Pallas kernels  5.26 us (10%)
  waiting for transfers between devices  4.19 us (8%)
  local copies, waits for them, and re-layouts  0.66 us (1%)
    ppermute x11, starting transfers between devices, swap(): lax.ppermute(value, ('grp', 'rep'), [(i, i ^ bit) for i in range(DEVICES)])  21.2 us
    all_to_all x1, blocking collectives, on_device(): lax.all_to_all(parcel, 'grp', 0, 0, axis_index_groups=QUARTERS, tiled=True)  19.4 us
    ppermute x11, waiting for transfers between devices, swap(): lax.ppermute(value, ('grp', 'rep'), [(i, i ^ bit) for i in range(DEVICES)])  4.19 us
    pallas_call x1, Pallas kernels, forward(): rate_kernel(forward_kernel, 'forward', [ROWS] * 2, [HBM, HBM, VMEM, VMEM,...  2.69 us
    pallas_call x1, Pallas kernels, spread(): rate_kernel(spread_kernel, 'spread', outs, [HBM] * 4, [own, padded], [plt...  2.57 us
  transfers between devices with their start and end apart: 11, of which 4 were waited for; matrix products, arithmetic and copies ran while one was open for 0% of the time, Pallas kernels for 5%

profile of v3, /device:TPU:1, one launch (start us, length us, event | category | flops | bytes accessed | tf_op | source)
XLA Modules:
  0.0 51.0 jit_solution(571301271315298601)
XLA Ops:
  0.0 0.0 copy-start
  0.0 2.6 %spread.1 = (f32[384,128]{1,0:T(8,128)S(1)}, f32[384,128]{1,0:T(8,128)S(1)}) custom-call(s32[1,4]{1,0:T(1,128)} %bitcast.14, s32[4,5]{1,0:T(4,128)} %partner_hbm.3, f32[6,4,256]{2,1,0:T(4,128)} %bitcast.9, f32[4,5,256,256]{3,2,1,0:T(8,128)} %rates.3), custom_call_target="tpu_custom_call" | custom-call | flops 62914560 | bytes 10485760 | tf_op jit(solution)/shard_map/spread/pallas_call | solution.py:197
  2.6 0.0 copy-start.1
  2.6 0.0 copy-start.2
  2.6 3.6 %collective-permute-start = (f32[384,128]{1,0:T(8,128)S(1)}, f32[384,128]{1,0:T(8,128)S(1)}, u32[]{:S(2)}, u32[]{:S(2)}) collective-permute-start(f32[384,128]{1,0:T(8,128)S(1)} %get-tuple-element.10), channel_id=1, source_target_pairs={{0,1},{1,0},{2,3},{3,2},{4,5},{5,4},{6,7},{7,6},{8,9},{9,8},{10,11... | collective-permute-start | bytes 589832 | tf_op jit(solution)/shard_map/ppermute | solution.py:22
  6.2 0.0 copy-done
  6.2 0.5 %collective-permute-start.3 = (f32[6,4,256]{2,1,0:T(4,128)S(1)}, f32[6,4,256]{2,1,0:T(4,128)S(1)}, u32[]{:S(2)}, u32[]{:S(2)}) collective-permute-start(f32[6,4,256]{2,1,0:T(4,128)S(1)} %bitcast.10), channel_id=1, source_target_pairs={{0,64},{1,65},{2,66},{3,67},{4,68},{5,69},{6,70},{7,71},{8,72},{9,... | collective-permute-start | bytes 73736 | tf_op jit(solution)/shard_map/ppermute | solution.py:22
  6.7 0.0 collective-permute-start.2
  6.7 3.6 %collective-permute-start.1 = (f32[6,4,256]{2,1,0:T(4,128)S(1)}, f32[6,4,256]{2,1,0:T(4,128)S(1)}, u32[]{:S(2)}, u32[]{:S(2)}) collective-permute-start(f32[6,4,256]{2,1,0:T(4,128)S(1)} %bitcast.12), channel_id=1, source_target_pairs={{0,192},{1,193},{2,194},{3,195},{4,196},{5,197},{6,198},{7,199},{8... | collective-permute-start | bytes 73736 | tf_op jit(solution)/shard_map/ppermute | solution.py:22
  10.4 0.0 collective-permute-done.3
  10.4 0.0 collective-permute-done.2
  10.4 1.4 %collective-permute-done.1 = f32[6,4,256]{2,1,0:T(4,128)S(1)} collective-permute-done((f32[6,4,256]{2,1,0:T(4,128)S(1)}, f32[6,4,256]{2,1,0:T(4,128)S(1)}, u32[]{:S(2)}, u32[]{:S(2)}) %collective-permute-start.1) | collective-permute-done | bytes 24608 | tf_op jit(solution)/shard_map/ppermute | solution.py:22
  11.9 0.0 collective-permute-done
  12.0 19.4 %all_to_all.5 = f32[16,48,128]{2,1,0:T(8,128)S(1)} all-to-all(f32[16,48,128]{2,1,0:T(8,128)S(1)} %pad_maximum_fusion), channel_id=1, replica_groups={{0,4,8,12,16,20,24,28,32,36,40,44,48,52,56,60},{64,68,72,76,80,84,88,92..., dimensions={0} | all-to-all | bytes 786432 | tf_op jit(solution)/shard_map/all_to_all | solution.py:233
  31.4 2.9 %collective-permute-start.4 = (f32[384,128]{1,0:T(8,128)S(1)}, f32[384,128]{1,0:T(8,128)S(1)}, u32[]{:S(2)}, u32[]{:S(2)}) collective-permute-start(f32[384,128]{1,0:T(8,128)S(1)} %bitcast.6), channel_id=1, source_target_pairs={{0,1},{1,0},{2,3},{3,2},{4,5},{5,4},{6,7},{7,6},{8,9},{9,8},{10,11... | collective-permute-start | bytes 589832 | tf_op jit(solution)/shard_map/ppermute | solution.py:22
  34.3 1.4 %collective-permute-start.8 = (f32[24,128]{1,0:T(8,128)S(1)}, f32[24,128]{1,0:T(8,128)S(1)}, u32[]{:S(2)}, u32[]{:S(2)}) collective-permute-start(f32[24,128]{1,0:T(8,128)S(1)} %get-tuple-element.14), channel_id=1, source_target_pairs={{0,128},{1,129},{2,130},{3,131},{4,132},{5,133},{6,134},{7,135},{8... | collective-permute-start | bytes 36872 | tf_op jit(solution)/shard_map/ppermute | solution.py:22
  35.7 1.8 %collective-permute-start.7 = (f32[24,128]{1,0:T(8,128)S(1)}, f32[24,128]{1,0:T(8,128)S(1)}, u32[]{:S(2)}, u32[]{:S(2)}) collective-permute-start(f32[24,128]{1,0:T(8,128)S(1)} %get-tuple-element.14), channel_id=1, source_target_pairs={{0,64},{1,65},{2,66},{3,67},{4,68},{5,69},{6,70},{7,71},{8,72},{9,... | collective-permute-start | bytes 36872 | tf_op jit(solution)/shard_map/ppermute | solution.py:22
  37.5 1.0 %collective-permute-start.6 = (f32[24,128]{1,0:T(8,128)S(1)}, f32[24,128]{1,0:T(8,128)S(1)}, u32[]{:S(2)}, u32[]{:S(2)}) collective-permute-start(f32[24,128]{1,0:T(8,128)S(1)} %get-tuple-element.14), channel_id=1, source_target_pairs={{0,192},{1,193},{2,194},{3,195},{4,196},{5,197},{6,198},{7,199},{8... | collective-permute-start | bytes 36872 | tf_op jit(solution)/shard_map/ppermute | solution.py:22
  38.5 0.0 collective-permute-done.4.other
  38.5 2.7 %forward.1 = (f32[24,128]{1,0:T(8,128)S(1)}, f32[24,128]{1,0:T(8,128)S(1)}) custom-call(s32[1,4]{1,0:T(1,128)} %bitcast.15, s32[4,5]{1,0:T(4,128)} %partner_hbm.3, f32[384,128]{1,0:T(8,128)S(1)} %bitcast.7, f32[384,128]{1,0:T(8,128)S(1)} %collective-permute-done.4.other, f32[4,5,256,256]{3,2,1,0:T(8,128)} %rates.3), custom_call_target="tpu_custom_call" | custom-call | flops 62914560 | bytes 10485760 | tf_op jit(solution)/shard_map/forward/pallas_call | solution.py:205
  41.2 1.5 %collective-permute-start.5 = (f32[24,128]{1,0:T(8,128)S(1)}, f32[24,128]{1,0:T(8,128)S(1)}, u32[]{:S(2)}, u32[]{:S(2)}) collective-permute-start(f32[24,128]{1,0:T(8,128)S(1)} %get-tuple-element.12), channel_id=1, source_target_pairs={{0,1},{1,0},{2,3},{3,2},{4,5},{5,4},{6,7},{7,6},{8,9},{9,8},{10,11... | collective-permute-start | bytes 36872 | tf_op jit(solution)/shard_map/ppermute | solution.py:22
  42.7 0.0 collective-permute-done.8
  42.8 0.0 collective-permute-done.7
  42.8 0.0 collective-permute-done.6
  42.8 0.8 %collective-permute-done.5 = f32[24,128]{1,0:T(8,128)S(1)} collective-permute-done((f32[24,128]{1,0:T(8,128)S(1)}, f32[24,128]{1,0:T(8,128)S(1)}, u32[]{:S(2)}, u32[]{:S(2)}) %collective-permute-start.5) | collective-permute-done | bytes 12320 | tf_op jit(solution)/shard_map/ppermute | solution.py:22
  43.6 3.0 %collective-permute-start.9 = (f32[24,128]{1,0:T(8,128)S(1)}, f32[24,128]{1,0:T(8,128)S(1)}, u32[]{:S(2)}, u32[]{:S(2)}) collective-permute-start(f32[24,128]{1,0:T(8,128)S(1)} %select_add_fusion), channel_id=1, source_target_pairs={{0,2},{1,3},{2,0},{3,1},{4,6},{5,7},{6,4},{7,5},{8,10},{9,11},{10,... | collective-permute-start | bytes 36872 | tf_op jit(solution)/shard_map/ppermute | solution.py:22
  46.6 1.1 %collective-permute-done.9 = f32[24,128]{1,0:T(8,128)S(1)} collective-permute-done((f32[24,128]{1,0:T(8,128)S(1)}, f32[24,128]{1,0:T(8,128)S(1)}, u32[]{:S(2)}, u32[]{:S(2)}) %collective-permute-start.9) | collective-permute-done | bytes 12320 | tf_op jit(solution)/shard_map/ppermute | solution.py:22
  47.7 1.8 %collective-permute-start.10 = (f32[24,128]{1,0:T(8,128)S(1)}, f32[24,128]{1,0:T(8,128)S(1)}, u32[]{:S(2)}, u32[]{:S(2)}) collective-permute-start(f32[24,128]{1,0:T(8,128)S(1)} %add.40), channel_id=1, source_target_pairs={{0,1},{1,0},{2,3},{3,2},{4,5},{5,4},{6,7},{7,6},{8,9},{9,8},{10,11... | collective-permute-start | bytes 36872 | tf_op jit(solution)/shard_map/ppermute | solution.py:22
  49.5 0.8 %collective-permute-done.10 = f32[24,128]{1,0:T(8,128)S(1)} collective-permute-done((f32[24,128]{1,0:T(8,128)S(1)}, f32[24,128]{1,0:T(8,128)S(1)}, u32[]{:S(2)}, u32[]{:S(2)}) %collective-permute-start.10) | collective-permute-done | bytes 12320 | tf_op jit(solution)/shard_map/ppermute | solution.py:22
  50.4 0.0 copy-done.1
  50.4 0.0 copy-done.2
  50.4 0.6 %copy.10 = f32[4,6,256]{2,0,1:T(4,128)} copy(f32[4,6,256]{2,1,0:T(8,128)S(1)} %copy_add_fusion) | data formatting | bytes 49152 | tf_op jit(solution)/shard_map/add | solution.py:243
  (13 shorter events, 0.2 us)
Async XLA Ops:
  0.0 6.2 %copy-start = (f32[4,6,256]{2,0,1:T(4,128)S(1)}, f32[4,6,256]{2,0,1:T(4,128)}, u32[]{:S(2)}) copy-start(f32[4,6,256]{2,0,1:T(4,128)} %param.6) | copy-start | bytes 73732
  2.6 47.8 %copy-start.1 = (f32[4,6,256]{2,0,1:T(4,128)S(1)}, f32[4,6,256]{2,0,1:T(4,128)}, u32[]{:S(2)}) copy-start(f32[4,6,256]{2,0,1:T(4,128)} %param.7) | copy-start | bytes 73732
  2.6 47.8 %copy-start.2 = (f32[4,256]{1,0:T(4,128)S(1)}, f32[4,256]{1,0:T(4,128)}, u32[]{:S(2)}) copy-start(f32[4,256]{1,0:T(4,128)} %param.8) | copy-start | bytes 12292
  2.6 9.3 %collective-permute-start = (f32[384,128]{1,0:T(8,128)S(1)}, f32[384,128]{1,0:T(8,128)S(1)}, u32[]{:S(2)}, u32[]{:S(2)}) collective-permute-start(f32[384,128]{1,0:T(8,128)S(1)} %get-tuple-element.10), channel_id=1, source_target_pairs={{0,1},{1,0},{2,3},{3,2},{4,5},{5,4},{6,7},{7,6},{8,9},{9,8},{10,11... | collective-permute-start | bytes 589832 | tf_op jit(solution)/shard_map/ppermute | solution.py:22
  6.2 4.2 %collective-permute-start.3 = (f32[6,4,256]{2,1,0:T(4,128)S(1)}, f32[6,4,256]{2,1,0:T(4,128)S(1)}, u32[]{:S(2)}, u32[]{:S(2)}) collective-permute-start(f32[6,4,256]{2,1,0:T(4,128)S(1)} %bitcast.10), channel_id=1, source_target_pairs={{0,64},{1,65},{2,66},{3,67},{4,68},{5,69},{6,70},{7,71},{8,72},{9,... | collective-permute-start | bytes 73736 | tf_op jit(solution)/shard_map/ppermute | solution.py:22
  6.7 3.7 %collective-permute-start.2 = (f32[6,4,256]{2,1,0:T(4,128)S(1)}, f32[6,4,256]{2,1,0:T(4,128)S(1)}, u32[]{:S(2)}, u32[]{:S(2)}) collective-permute-start(f32[6,4,256]{2,1,0:T(4,128)S(1)} %bitcast.11), channel_id=1, source_target_pairs={{0,128},{1,129},{2,130},{3,131},{4,132},{5,133},{6,134},{7,135},{8... | collective-permute-start | bytes 73736 | tf_op jit(solution)/shard_map/ppermute | solution.py:22
  6.7 5.1 %collective-permute-start.1 = (f32[6,4,256]{2,1,0:T(4,128)S(1)}, f32[6,4,256]{2,1,0:T(4,128)S(1)}, u32[]{:S(2)}, u32[]{:S(2)}) collective-permute-start(f32[6,4,256]{2,1,0:T(4,128)S(1)} %bitcast.12), channel_id=1, source_target_pairs={{0,192},{1,193},{2,194},{3,195},{4,196},{5,197},{6,198},{7,199},{8... | collective-permute-start | bytes 73736 | tf_op jit(solution)/shard_map/ppermute | solution.py:22
  31.4 7.1 %collective-permute-start.4 = (f32[384,128]{1,0:T(8,128)S(1)}, f32[384,128]{1,0:T(8,128)S(1)}, u32[]{:S(2)}, u32[]{:S(2)}) collective-permute-start(f32[384,128]{1,0:T(8,128)S(1)} %bitcast.6), channel_id=1, source_target_pairs={{0,1},{1,0},{2,3},{3,2},{4,5},{5,4},{6,7},{7,6},{8,9},{9,8},{10,11... | collective-permute-start | bytes 589832 | tf_op jit(solution)/shard_map/ppermute | solution.py:22
  34.3 8.4 %collective-permute-start.8 = (f32[24,128]{1,0:T(8,128)S(1)}, f32[24,128]{1,0:T(8,128)S(1)}, u32[]{:S(2)}, u32[]{:S(2)}) collective-permute-start(f32[24,128]{1,0:T(8,128)S(1)} %get-tuple-element.14), channel_id=1, source_target_pairs={{0,128},{1,129},{2,130},{3,131},{4,132},{5,133},{6,134},{7,135},{8... | collective-permute-start | bytes 36872 | tf_op jit(solution)/shard_map/ppermute | solution.py:22
  35.7 7.1 %collective-permute-start.7 = (f32[24,128]{1,0:T(8,128)S(1)}, f32[24,128]{1,0:T(8,128)S(1)}, u32[]{:S(2)}, u32[]{:S(2)}) collective-permute-start(f32[24,128]{1,0:T(8,128)S(1)} %get-tuple-element.14), channel_id=1, source_target_pairs={{0,64},{1,65},{2,66},{3,67},{4,68},{5,69},{6,70},{7,71},{8,72},{9,... | collective-permute-start | bytes 36872 | tf_op jit(solution)/shard_map/ppermute | solution.py:22
  37.5 5.3 %collective-permute-start.6 = (f32[24,128]{1,0:T(8,128)S(1)}, f32[24,128]{1,0:T(8,128)S(1)}, u32[]{:S(2)}, u32[]{:S(2)}) collective-permute-start(f32[24,128]{1,0:T(8,128)S(1)} %get-tuple-element.14), channel_id=1, source_target_pairs={{0,192},{1,193},{2,194},{3,195},{4,196},{5,197},{6,198},{7,199},{8... | collective-permute-start | bytes 36872 | tf_op jit(solution)/shard_map/ppermute | solution.py:22
  41.2 2.4 %collective-permute-start.5 = (f32[24,128]{1,0:T(8,128)S(1)}, f32[24,128]{1,0:T(8,128)S(1)}, u32[]{:S(2)}, u32[]{:S(2)}) collective-permute-start(f32[24,128]{1,0:T(8,128)S(1)} %get-tuple-element.12), channel_id=1, source_target_pairs={{0,1},{1,0},{2,3},{3,2},{4,5},{5,4},{6,7},{7,6},{8,9},{9,8},{10,11... | collective-permute-start | bytes 36872 | tf_op jit(solution)/shard_map/ppermute | solution.py:22
  43.6 4.1 %collective-permute-start.9 = (f32[24,128]{1,0:T(8,128)S(1)}, f32[24,128]{1,0:T(8,128)S(1)}, u32[]{:S(2)}, u32[]{:S(2)}) collective-permute-start(f32[24,128]{1,0:T(8,128)S(1)} %select_add_fusion), channel_id=1, source_target_pairs={{0,2},{1,3},{2,0},{3,1},{4,6},{5,7},{6,4},{7,5},{8,10},{9,11},{10,... | collective-permute-start | bytes 36872 | tf_op jit(solution)/shard_map/ppermute | solution.py:22
  47.7 2.6 %collective-permute-start.10 = (f32[24,128]{1,0:T(8,128)S(1)}, f32[24,128]{1,0:T(8,128)S(1)}, u32[]{:S(2)}, u32[]{:S(2)}) collective-permute-start(f32[24,128]{1,0:T(8,128)S(1)} %add.40), channel_id=1, source_target_pairs={{0,1},{1,0},{2,3},{3,2},{4,5},{5,4},{6,7},{7,6},{8,9},{9,8},{10,11... | collective-permute-start | bytes 36872 | tf_op jit(solution)/shard_map/ppermute | solution.py:22

commit v4 on v3

v4 whole, which is shorter than its diff:
```python
import jax
import jax.numpy as jnp
from jax import lax
from jax.experimental import pallas as pl
from jax.experimental.pallas import tpu as pltpu
from jax.sharding import PartitionSpec as P

Y_LO, X_HIGH, X_LOW, Y_HI, CORE = 128, 64, 32, 2, 1
MIRROR = X_HIGH + X_LOW
QUARTER_BITS = Y_LO + MIRROR
DEVICES = 256
BLOCKS, SLOTS, COMPONENTS, STATES, HALF = 4, 5, 6, 256, 128
PAIRS = BLOCKS * SLOTS
UNROLL = 4
PHONON = 64
FIRST_PHONON = 192
ROWS = BLOCKS * COMPONENTS
OWNERS = PHONON // BLOCKS
QUARTERS = [[quarter * OWNERS + owner for owner in range(OWNERS)] for quarter in range(4)]


def swap(value, bit):
    return lax.ppermute(value, ("grp", "rep"), [(i, i ^ bit) for i in range(DEVICES)])


def from_phonon(value, bits):
    pairs = [(i, i ^ bits) for i in range(DEVICES) if i & QUARTER_BITS == QUARTER_BITS]
    return lax.ppermute(value, ("grp", "rep"), pairs)


def to_phonon(value, bits):
    pairs = [(i ^ bits, i) for i in range(DEVICES) if i & QUARTER_BITS == QUARTER_BITS]
    return lax.ppermute(value, ("grp", "rep"), pairs)


def split(value):
    high = value.astype(jnp.bfloat16)
    low = (value - high.astype(jnp.float32)).astype(jnp.bfloat16)
    return high, low


def stack_split(value):
    high, low = split(value)
    both = jnp.concatenate([high.astype(jnp.float32), low.astype(jnp.float32)], axis=0)
    return high, both.astype(jnp.bfloat16)


def multiply(high, both, rates_high, rates_low, contract):
    dims = (((1,), (contract,)), ((), ()))
    main = lax.dot_general(both, rates_high, dims, preferred_element_type=jnp.float32)
    rest = lax.dot_general(high, rates_low, dims, preferred_element_type=jnp.float32)
    return main[:8] + main[8:] + rest


def product(high, both, weights, contract):
    return multiply(high, both, *split(weights), contract)


def rate_copies(count_hbm, partner_hbm, rates, count, partner, held, sems, small_sems, meanwhile):
    def fetch(block, slot):
        pair = block * SLOTS + slot
        return pltpu.make_async_copy(rates.at[block, slot], held.at[pair], sems.at[pair])

    counts = pltpu.make_async_copy(count_hbm, count, small_sems.at[0])
    partners = pltpu.make_async_copy(partner_hbm, partner, small_sems.at[1])
    counts.start()
    partners.start()
    for block in range(BLOCKS):
        fetch(block, 0).start()
    meanwhile()
    counts.wait()
    for block in range(BLOCKS):

        @pl.loop(1, count[0, block])
        def _(slot):
            fetch(block, slot).start()

    partners.wait()
    return fetch


def visit_live(count, chosen, fetch, visit):
    total = jnp.int32(0)
    for block in range(BLOCKS):

        def note(slot, at):
            chosen[at] = block * SLOTS + slot
            return at + 1

        total = lax.fori_loop(0, count[0, block], note, total)

    @pl.loop(0, lax.div(total + (UNROLL - 1), UNROLL))
    def _(step):
        places = [step * UNROLL + offset for offset in range(UNROLL)]
        pairs = [chosen[jnp.minimum(place, total - 1)] for place in places]
        blocks = [lax.div(pair, SLOTS) for pair in pairs]
        slots = [pair - SLOTS * block for pair, block in zip(pairs, blocks)]
        for place, block, slot in zip(places, blocks, slots):

            if fetch is not None:

                @pl.when(place < total)
                def _():
                    fetch(block, slot).wait()

        visit([(block, slot, place < total) for block, slot, place in zip(blocks, slots, places)])


def spread_kernel(
    count_hbm, partner_hbm, deviation, rates, keep, give, own, rows, held, count, partner, chosen, own_sem, sems, small
):
    core = lax.rem(lax.axis_index("rep"), 2)

    def clear():
        keep[...] = jnp.zeros_like(keep)
        give[...] = jnp.zeros_like(give)

    @pl.when(lax.axis_index("grp") >= 3 * OWNERS)
    def _():
        clear()

    @pl.when(lax.axis_index("grp") < 3 * OWNERS)
    def _():
        own_copy = pltpu.make_async_copy(deviation, own, own_sem)
        own_copy.start()
        fetch = rate_copies(
            count_hbm, partner_hbm, rates, count, partner, held, sems, small, clear
        )
        own_copy.wait()
        for block in range(BLOCKS):
            parts = [own[component, block : block + 1, :] for component in range(COMPONENTS)]
            rows[block] = jnp.concatenate(parts + [jnp.zeros((2, STATES), jnp.float32)], axis=0)

        def visit(some):
            values = []
            for block, slot, live in some:
                high, both = stack_split(jnp.where(live, rows[block], 0.0))
                values.append(product(high, both, held[block * SLOTS + slot], 0)[:COMPONENTS])
            for (block, slot, live), value in zip(some, values):
                left, right = value[:, :HALF], value[:, HALF:]
                row = (partner[block, slot] - FIRST_PHONON) * COMPONENTS
                keep[pl.ds(row, COMPONENTS), :] += jnp.where(core == 0, left, right)
                give[pl.ds(row, COMPONENTS), :] += jnp.where(core == 0, right, left)

        visit_live(count, chosen, fetch, visit)


def prepare_kernel(count_hbm, partner_hbm, rates, high, low, token, held, count, partner, chosen, sems, small):
    def clear():
        token[...] = jnp.zeros_like(token)

    fetch = rate_copies(
        count_hbm, partner_hbm, rates, count, partner, held, sems, small, clear
    )

    def visit(some):
        for block, slot, _ in some:
            pair = block * SLOTS + slot
            high[pair], low[pair] = split(held[pair])

    visit_live(count, chosen, fetch, visit)


def forward_kernel(count_hbm, partner_hbm, mine, other, high_ref, low_ref, drag, out, totals, count, partner, chosen, small):
    core = lax.rem(lax.axis_index("rep"), 2)
    counts = pltpu.make_async_copy(count_hbm, count, small.at[0])
    partners = pltpu.make_async_copy(partner_hbm, partner, small.at[1])
    counts.start()
    partners.start()
    totals[...] = jnp.zeros_like(totals)
    counts.wait()
    partners.wait()

    def visit(some):
        values = []
        for block, slot, live in some:
            row = (partner[block, slot] - FIRST_PHONON) * COMPONENTS
            near, far = mine[pl.ds(row, COMPONENTS), :], other[pl.ds(row, COMPONENTS), :]
            left, right = jnp.where(core == 0, near, far), jnp.where(core == 0, far, near)
            picked = jnp.concatenate([left, right], axis=1)
            padded = jnp.concatenate([picked, jnp.zeros((2, STATES), jnp.float32)], axis=0)
            high, both = stack_split(jnp.where(live, padded, 0.0))
            pair = block * SLOTS + slot
            values.append(multiply(high, both, high_ref[pair], low_ref[pair], 1))
        for (block, slot, live), value in zip(some, values):
            totals[block] += value

    visit_live(count, chosen, None, visit)
    for block in range(BLOCKS):
        own = drag[block * COMPONENTS : (block + 1) * COMPONENTS, :]
        for half in range(2):
            first = half * ROWS + block * COMPONENTS
            value = totals[block, :COMPONENTS, half * HALF : (half + 1) * HALF]
            out[first : first + COMPONENTS, :] = value + jnp.where(core == half, own, 0.0)


VMEM = pl.BlockSpec(memory_space=pltpu.VMEM)
HBM = pl.BlockSpec(memory_space=pltpu.HBM)
HELD = pltpu.VMEM((PAIRS, STATES, STATES), jnp.float32)
LISTS = [
    pltpu.SMEM((1, BLOCKS), jnp.int32),
    pltpu.SMEM((BLOCKS, SLOTS), jnp.int32),
    pltpu.SMEM((PAIRS,), jnp.int32),
]
RATE_SEMS = pltpu.SemaphoreType.DMA((PAIRS,))
SMALL_SEMS = pltpu.SemaphoreType.DMA((2,))


def rate_kernel(body, name, outs, in_specs, scratch):
    return pl.pallas_call(
        body,
        name=name,
        out_shape=outs,
        in_specs=in_specs,
        out_specs=[VMEM] * len(outs),
        scratch_shapes=scratch,
        compiler_params=pltpu.CompilerParams(vmem_limit_bytes=16 * 1024 * 1024),
        cost_estimate=pl.CostEstimate(
            flops=6 * PAIRS * 8 * STATES * STATES,
            bytes_accessed=2 * PAIRS * STATES * STATES * 4,
            transcendentals=0,
        ),
    )


def in_hbm(*values):
    return [pltpu.with_memory_space_constraint(value, pltpu.HBM) for value in values]


def float_rows(rows):
    return jax.ShapeDtypeStruct((rows, HALF), jnp.float32)


def spread(count, partner, deviation, rates):
    own = pltpu.VMEM((COMPONENTS, BLOCKS, STATES), jnp.float32)
    padded = pltpu.VMEM((BLOCKS, 8, STATES), jnp.float32)
    scratch = [own, padded, HELD] + LISTS + [pltpu.SemaphoreType.DMA, RATE_SEMS, SMALL_SEMS]
    return rate_kernel(
        spread_kernel, "spread", [float_rows(PHONON * COMPONENTS)] * 2, [HBM] * 4, scratch
    )(*in_hbm(count, partner, deviation, rates))


def prepare(count, partner, rates):
    terms = [jax.ShapeDtypeStruct((PAIRS, STATES, STATES), jnp.bfloat16)] * 2
    scratch = [HELD] + LISTS + [RATE_SEMS, SMALL_SEMS]
    return rate_kernel(prepare_kernel, "prepare", terms + [float_rows(8)], [HBM] * 3, scratch)(
        *in_hbm(count, partner, rates)
    )


def forward(count, partner, mine, other, high, low, drag):
    totals = pltpu.VMEM((BLOCKS, 8, STATES), jnp.float32)
    return rate_kernel(
        forward_kernel,
        "forward",
        [float_rows(2 * ROWS)],
        [pl.BlockSpec(memory_space=pl.ANY)] * 2 + [VMEM] * 5,
        [totals] + LISTS + [SMALL_SEMS],
    )(count, partner, mine, other, high, low, drag)[0]


def on_device(deviation, source, lifetime, rates, partner, count):
    core = lax.axis_index("rep") % 2
    quarter = lax.axis_index("grp") // OWNERS
    is_phonon = quarter == 3
    live = count.T
    turned = deviation.transpose(1, 0, 2)

    own = lax.dynamic_slice_in_dim(turned, core * HALF, HALF, 2)
    own = own.transpose(1, 0, 2).reshape(1, ROWS, HALF)

    keep, give = spread(live, partner, turned, rates)
    drag = (keep + swap(give, CORE)).reshape(OWNERS, ROWS, HALF)
    half = OWNERS // 2
    drag = jnp.where(quarter % 2 == 1, drag, jnp.concatenate([drag[half:], drag[:half]]))

    parcel = jnp.where(is_phonon, own, drag)
    arrived = lax.all_to_all(parcel, "grp", 0, 0, axis_index_groups=QUARTERS, tiled=True)
    arrived, live = lax.optimization_barrier((arrived, live))
    rates_high, rates_low, token = prepare(live, partner, rates)
    drag = arrived.sum(0)
    gathered = arrived.reshape(PHONON * COMPONENTS, HALF)
    spare = jnp.zeros((PHONON * COMPONENTS - ROWS, HALF), jnp.float32)
    outgoing = jnp.where(is_phonon, gathered, jnp.concatenate([drag, spare]))
    incoming = [swap(outgoing, bits) for bits in (QUARTER_BITS, MIRROR, Y_LO)]
    drag = incoming[0][:ROWS] + incoming[1][:ROWS] + incoming[2][:ROWS]
    phonon = jnp.where(quarter == 0, incoming[0], jnp.where(quarter == 1, incoming[2], incoming[1]))
    phonon = jnp.where(is_phonon, gathered, phonon)
    phonon, token = lax.optimization_barrier((phonon, swap(token, CORE)))
    drag = jnp.where(is_phonon, drag + token[:1], 0.0)
    total = forward(live, partner, phonon, swap(phonon, CORE), rates_high, rates_low, drag)
    total = total + swap(total, CORE)
    total = total + swap(total, Y_HI)
    total = total.reshape(2, BLOCKS, COMPONENTS, HALF)
    summed = jnp.concatenate([total[0], total[1]], axis=-1)
    return source + lifetime[:, None, :] * summed


def solution(mesh):
    placed = (
        P("grp", None, None),
        P("grp", None, None),
        P("grp", None),
        P("grp", "rep", None, None),
        P("grp", "rep"),
        P("grp", "rep"),
    )
    return jax.shard_map(
        on_device, mesh=mesh, in_specs=placed, out_specs=P("grp", None, None), check_vma=False
    )
```

time: 51.2 us -> 46.2 us (0.902)
  blocking collectives: 19.4 us -> 14.8 us
  starting transfers between devices: 21.2 us -> 17.6 us
  waiting for transfers between devices: 4.19 us -> 5.78 us
  Pallas kernels: 5.26 us -> 6.47 us
    all_to_all x1, blocking collectives: 19.4 us -> 14.8 us  [on_device(): lax.all_to_all(parcel, 'grp', 0, 0, axis_index_groups=QUARTERS, tiled=True)]
    ppermute x11 -> x8, starting transfers between devices: 21.2 us -> 17.6 us  [swap(): lax.ppermute(value, ('grp', 'rep'), [(i, i ^ bit) for i in range(DEVICES)])]
    ppermute x11 -> x8, waiting for transfers between devices: 4.19 us -> 5.78 us  [swap(): lax.ppermute(value, ('grp', 'rep'), [(i, i ^ bit) for i in range(DEVICES)])]
    pallas_call x2 -> x3, Pallas kernels: 5.26 us -> 6.47 us  [the longest x1 2.56 us: spread(): rate_kernel(spread_kernel, 'spread', [float_rows(PHONON * COMPONENTS)] *...]
  transfers between devices with their start and end apart: 11 -> 8, of which waited for: 4 -> 5; matrix products, arithmetic and copies ran while one was open for 0% -> 0% of each run, Pallas kernels for 5% -> 5%
where the time goes in v4:
time: 46.2 us; the launch traced here: 45.7 us
  starting transfers between devices  17.6 us (38%)
  blocking collectives  14.8 us (32%)
  Pallas kernels  6.47 us (14%)
  waiting for transfers between devices  5.78 us (13%)
  local copies, waits for them, and re-layouts  0.69 us (1%)
    ppermute x8, starting transfers between devices, swap(): lax.ppermute(value, ('grp', 'rep'), [(i, i ^ bit) for i in range(DEVICES)])  17.6 us
    all_to_all x1, blocking collectives, on_device(): lax.all_to_all(parcel, 'grp', 0, 0, axis_index_groups=QUARTERS, tiled=True)  14.8 us
    ppermute x8, waiting for transfers between devices, swap(): lax.ppermute(value, ('grp', 'rep'), [(i, i ^ bit) for i in range(DEVICES)])  5.78 us
    pallas_call x1, Pallas kernels, spread(): rate_kernel(spread_kernel, 'spread', [float_rows(PHONON * COMPONENTS)] *...  2.56 us
    pallas_call x1, Pallas kernels, prepare(): rate_kernel(prepare_kernel, 'prepare', terms + [float_rows(8)], [HBM] * 3...  2.45 us
    pallas_call x1, Pallas kernels, forward(): rate_kernel(forward_kernel, 'forward', [float_rows(2 * ROWS)], [pl.BlockS...  1.46 us
  transfers between devices with their start and end apart: 8, of which 5 were waited for; matrix products, arithmetic and copies ran while one was open for 0% of the time, Pallas kernels for 5%

profile of v4, /device:TPU:1, one launch (start us, length us, event | category | flops | bytes accessed | tf_op | source)
XLA Modules:
  0.0 45.7 jit_solution(12360153258203792991)
XLA Ops:
  0.0 0.0 copy-start.2
  0.0 2.6 %spread.1 = (f32[384,128]{1,0:T(8,128)S(1)}, f32[384,128]{1,0:T(8,128)S(1)}) custom-call(s32[1,4]{1,0:T(1,128)} %bitcast.10, s32[4,5]{1,0:T(4,128)} %partner_hbm.5, f32[6,4,256]{2,1,0:T(4,128)} %bitcast.16, f32[4,5,256,256]{3,2,1,0:T(8,128)} %rates.3), custom_call_target="tpu_custom_call" | custom-call | flops 62914560 | bytes 10485760 | tf_op jit(solution)/shard_map/spread/pallas_call | solution.py:238
  2.6 3.6 %collective-permute-start = (f32[384,128]{1,0:T(8,128)S(1)}, f32[384,128]{1,0:T(8,128)S(1)}, u32[]{:S(2)}, u32[]{:S(2)}) collective-permute-start(f32[384,128]{1,0:T(8,128)S(1)} %get-tuple-element.15), channel_id=1, source_target_pairs={{0,1},{1,0},{2,3},{3,2},{4,5},{5,4},{6,7},{7,6},{8,9},{9,8},{10,11... | collective-permute-start | bytes 589832 | tf_op jit(solution)/shard_map/ppermute | solution.py:23
  6.2 0.0 copy-done.2
  6.2 1.0 %collective-permute-done = f32[384,128]{1,0:T(8,128)S(1)} collective-permute-done((f32[384,128]{1,0:T(8,128)S(1)}, f32[384,128]{1,0:T(8,128)S(1)}, u32[]{:S(2)}, u32[]{:S(2)}) %collective-permute-start) | collective-permute-done | bytes 196640 | tf_op jit(solution)/shard_map/ppermute | solution.py:23
  7.3 14.8 %all_to_all.5 = f32[16,24,128]{2,1,0:T(8,128)S(1)} all-to-all(f32[16,24,128]{2,1,0:T(8,128)S(1)} %fusion), channel_id=1, replica_groups={{0,4,8,12,16,20,24,28,32,36,40,44,48,52,56,60},{64,68,72,76,80,84,88,92..., dimensions={0} | all-to-all | bytes 393216 | tf_op jit(solution)/shard_map/all_to_all | solution.py:278
  22.2 1.9 %collective-permute-start.3 = (f32[384,128]{1,0:T(8,128)S(1)}, f32[384,128]{1,0:T(8,128)S(1)}, u32[]{:S(2)}, u32[]{:S(2)}) collective-permute-start(f32[384,128]{1,0:T(8,128)S(1)} %bitcast_select_fusion.1), channel_id=1, source_target_pairs={{0,96},{1,97},{2,98},{3,99},{4,100},{5,101},{6,102},{7,103},{8,104... | collective-permute-start | bytes 589832 | tf_op jit(solution)/shard_map/ppermute | solution.py:23
  24.1 0.0 collective-permute-start.2
  24.1 2.2 %collective-permute-start.1 = (f32[384,128]{1,0:T(8,128)S(1)}, f32[384,128]{1,0:T(8,128)S(1)}, u32[]{:S(2)}, u32[]{:S(2)}) collective-permute-start(f32[384,128]{1,0:T(8,128)S(1)} %bitcast_select_fusion.1), channel_id=1, source_target_pairs={{0,224},{1,225},{2,226},{3,227},{4,228},{5,229},{6,230},{7,231},{8... | collective-permute-start | bytes 589832 | tf_op jit(solution)/shard_map/ppermute | solution.py:23
  26.3 0.0 copy-start
  26.3 0.0 copy-start.1
  26.3 2.4 %prepare.1 = (bf16[20,256,256]{2,1,0:T(8,128)(2,1)S(1)}, bf16[20,256,256]{2,1,0:T(8,128)(2,1)S(1)}, f32[8,128]{1,0:T(8,128)S(1)}) custom-call(s32[1,4]{1,0:T(1,128)} %bitcast.11, s32[4,5]{1,0:T(4,128)} %partner_hbm.5, f32[4,5,256,256]{3,2,1,0:T(8,128)} %rates.3), custom_call_target="tpu_custom_call" | custom-call | flops 62914560 | bytes 10485760 | tf_op jit(solution)/shard_map/prepare/pallas_call | solution.py:246
  28.8 3.1 %collective-permute-start.4 = (f32[8,128]{1,0:T(8,128)S(1)}, f32[8,128]{1,0:T(8,128)S(1)}, u32[]{:S(2)}, u32[]{:S(2)}) collective-permute-start(f32[8,128]{1,0:T(8,128)S(1)} %get-tuple-element.18), channel_id=1, source_target_pairs={{0,1},{1,0},{2,3},{3,2},{4,5},{5,4},{6,7},{7,6},{8,9},{9,8},{10,11... | collective-permute-start | bytes 12296 | tf_op jit(solution)/shard_map/ppermute | solution.py:23
  31.9 0.0 collective-permute-done.3
  31.9 0.0 collective-permute-done.2
  31.9 1.1 %collective-permute-done.1 = f32[384,128]{1,0:T(8,128)S(1)} collective-permute-done((f32[384,128]{1,0:T(8,128)S(1)}, f32[384,128]{1,0:T(8,128)S(1)}, u32[]{:S(2)}, u32[]{:S(2)}) %collective-permute-start.1) | collective-permute-done | bytes 196640 | tf_op jit(solution)/shard_map/ppermute | solution.py:23
  33.0 0.0 collective-permute-done.4
  33.1 3.5 %collective-permute-start.5 = (f32[384,128]{1,0:T(8,128)S(1)}, f32[384,128]{1,0:T(8,128)S(1)}, u32[]{:S(2)}, u32[]{:S(2)}) collective-permute-start(f32[384,128]{1,0:T(8,128)S(1)} %bitcast_select_fusion.mine), channel_id=1, source_target_pairs={{0,1},{1,0},{2,3},{3,2},{4,5},{5,4},{6,7},{7,6},{8,9},{9,8},{10,11... | collective-permute-start | bytes 589832 | tf_op jit(solution)/shard_map/ppermute | solution.py:23
  36.5 1.1 %collective-permute-done.5.other = f32[384,128]{1,0:T(8,128)S(1)} collective-permute-done((f32[384,128]{1,0:T(8,128)S(1)}, f32[384,128]{1,0:T(8,128)S(1)}, u32[]{:S(2)}, u32[]{:S(2)}) %collective-permute-start.5) | collective-permute-done | bytes 196640 | tf_op jit(solution)/shard_map/ppermute | solution.py:23
  37.6 0.0 copy-done
  37.6 0.0 copy-done.1
  37.6 0.0 copy-start.3
  37.6 0.0 copy-start.4
  37.6 1.5 %forward.1 = f32[48,128]{1,0:T(8,128)S(1)} custom-call(s32[1,4]{1,0:T(1,128)S(1)} %bitcast.12, s32[4,5]{1,0:T(4,128)S(1)} %copy-done, f32[384,128]{1,0:T(8,128)S(1)} %bitcast_select_fusion.mine, f32[384,128]{1,0:T(8,128)S(1)} %collective-permute-done.5.other, bf16[20,256,256]{2,1,0:T(8,128)(2,1)S(1)} %get-tuple-element.20.high_ref, ...), custom_call_target="tpu_custom_call" | custom-call | flops 62914560 | bytes 10485760 | tf_op jit(solution)/shard_map/forward/pallas_call | solution.py:253
  39.1 0.9 %collective-permute-start.6 = (f32[48,128]{1,0:T(8,128)S(1)}, f32[48,128]{1,0:T(8,128)S(1)}, u32[]{:S(2)}, u32[]{:S(2)}) collective-permute-start(f32[48,128]{1,0:T(8,128)S(1)} %forward.1), channel_id=1, source_target_pairs={{0,1},{1,0},{2,3},{3,2},{4,5},{5,4},{6,7},{7,6},{8,9},{9,8},{10,11... | collective-permute-start | bytes 73736 | tf_op jit(solution)/shard_map/ppermute | solution.py:23
  40.0 0.8 %collective-permute-done.6 = f32[48,128]{1,0:T(8,128)S(1)} collective-permute-done((f32[48,128]{1,0:T(8,128)S(1)}, f32[48,128]{1,0:T(8,128)S(1)}, u32[]{:S(2)}, u32[]{:S(2)}) %collective-permute-start.6) | collective-permute-done | bytes 24608 | tf_op jit(solution)/shard_map/ppermute | solution.py:23
  40.8 2.5 %collective-permute-start.7 = (f32[48,128]{1,0:T(8,128)S(1)}, f32[48,128]{1,0:T(8,128)S(1)}, u32[]{:S(2)}, u32[]{:S(2)}) collective-permute-start(f32[48,128]{1,0:T(8,128)S(1)} %add.50), channel_id=1, source_target_pairs={{0,2},{1,3},{2,0},{3,1},{4,6},{5,7},{6,4},{7,5},{8,10},{9,11},{10,... | collective-permute-start | bytes 73736 | tf_op jit(solution)/shard_map/ppermute | solution.py:23
  43.3 1.7 %collective-permute-done.7 = f32[48,128]{1,0:T(8,128)S(1)} collective-permute-done((f32[48,128]{1,0:T(8,128)S(1)}, f32[48,128]{1,0:T(8,128)S(1)}, u32[]{:S(2)}, u32[]{:S(2)}) %collective-permute-start.7) | collective-permute-done | bytes 24608 | tf_op jit(solution)/shard_map/ppermute | solution.py:23
  45.0 0.0 copy-done.3
  45.0 0.0 copy-done.4
  45.1 0.6 %copy.11 = f32[4,6,256]{2,0,1:T(4,128)} copy(f32[4,6,256]{2,1,0:T(8,128)S(1)} %fusion.1) | data formatting | bytes 49152 | tf_op jit(solution)/shard_map/add | solution.py:296
  (17 shorter events, 0.2 us)
Async XLA Ops:
  0.0 6.2 %copy-start.2 = (f32[4,6,256]{2,0,1:T(4,128)S(1)}, f32[4,6,256]{2,0,1:T(4,128)}, u32[]{:S(2)}) copy-start(f32[4,6,256]{2,0,1:T(4,128)} %param.6) | copy-start | bytes 73732
  2.6 4.7 %collective-permute-start = (f32[384,128]{1,0:T(8,128)S(1)}, f32[384,128]{1,0:T(8,128)S(1)}, u32[]{:S(2)}, u32[]{:S(2)}) collective-permute-start(f32[384,128]{1,0:T(8,128)S(1)} %get-tuple-element.15), channel_id=1, source_target_pairs={{0,1},{1,0},{2,3},{3,2},{4,5},{5,4},{6,7},{7,6},{8,9},{9,8},{10,11... | collective-permute-start | bytes 589832 | tf_op jit(solution)/shard_map/ppermute | solution.py:23
  22.2 9.7 %collective-permute-start.3 = (f32[384,128]{1,0:T(8,128)S(1)}, f32[384,128]{1,0:T(8,128)S(1)}, u32[]{:S(2)}, u32[]{:S(2)}) collective-permute-start(f32[384,128]{1,0:T(8,128)S(1)} %bitcast_select_fusion.1), channel_id=1, source_target_pairs={{0,96},{1,97},{2,98},{3,99},{4,100},{5,101},{6,102},{7,103},{8,104... | collective-permute-start | bytes 589832 | tf_op jit(solution)/shard_map/ppermute | solution.py:23
  24.1 7.7 %collective-permute-start.2 = (f32[384,128]{1,0:T(8,128)S(1)}, f32[384,128]{1,0:T(8,128)S(1)}, u32[]{:S(2)}, u32[]{:S(2)}) collective-permute-start(f32[384,128]{1,0:T(8,128)S(1)} %bitcast_select_fusion.1), channel_id=1, source_target_pairs={{0,128},{1,129},{2,130},{3,131},{4,132},{5,133},{6,134},{7,135},{8... | collective-permute-start | bytes 589832 | tf_op jit(solution)/shard_map/ppermute | solution.py:23
  24.1 8.9 %collective-permute-start.1 = (f32[384,128]{1,0:T(8,128)S(1)}, f32[384,128]{1,0:T(8,128)S(1)}, u32[]{:S(2)}, u32[]{:S(2)}) collective-permute-start(f32[384,128]{1,0:T(8,128)S(1)} %bitcast_select_fusion.1), channel_id=1, source_target_pairs={{0,224},{1,225},{2,226},{3,227},{4,228},{5,229},{6,230},{7,231},{8... | collective-permute-start | bytes 589832 | tf_op jit(solution)/shard_map/ppermute | solution.py:23
  26.3 11.3 %copy-start = (s32[4,5]{1,0:T(4,128)S(1)}, s32[4,5]{1,0:T(4,128)}, u32[]{:S(2)}) copy-start(s32[4,5]{1,0:T(4,128)} %partner_hbm.5) | copy-start | bytes 244
  26.3 11.3 %copy-start.1 = (s32[4,1]{0,1:T(1,128)S(1)}, s32[4,1]{0,1:T(1,128)}, u32[]{:S(2)}) copy-start(s32[4,1]{0,1:T(1,128)} %param.11) | copy-start | bytes 52
  28.8 4.3 %collective-permute-start.4 = (f32[8,128]{1,0:T(8,128)S(1)}, f32[8,128]{1,0:T(8,128)S(1)}, u32[]{:S(2)}, u32[]{:S(2)}) collective-permute-start(f32[8,128]{1,0:T(8,128)S(1)} %get-tuple-element.18), channel_id=1, source_target_pairs={{0,1},{1,0},{2,3},{3,2},{4,5},{5,4},{6,7},{7,6},{8,9},{9,8},{10,11... | collective-permute-start | bytes 12296 | tf_op jit(solution)/shard_map/ppermute | solution.py:23
  33.1 4.5 %collective-permute-start.5 = (f32[384,128]{1,0:T(8,128)S(1)}, f32[384,128]{1,0:T(8,128)S(1)}, u32[]{:S(2)}, u32[]{:S(2)}) collective-permute-start(f32[384,128]{1,0:T(8,128)S(1)} %bitcast_select_fusion.mine), channel_id=1, source_target_pairs={{0,1},{1,0},{2,3},{3,2},{4,5},{5,4},{6,7},{7,6},{8,9},{9,8},{10,11... | collective-permute-start | bytes 589832 | tf_op jit(solution)/shard_map/ppermute | solution.py:23
  37.6 7.4 %copy-start.3 = (f32[4,6,256]{2,0,1:T(4,128)S(1)}, f32[4,6,256]{2,0,1:T(4,128)}, u32[]{:S(2)}) copy-start(f32[4,6,256]{2,0,1:T(4,128)} %param.7) | copy-start | bytes 73732
  37.6 7.4 %copy-start.4 = (f32[4,256]{1,0:T(4,128)S(1)}, f32[4,256]{1,0:T(4,128)}, u32[]{:S(2)}) copy-start(f32[4,256]{1,0:T(4,128)} %param.8) | copy-start | bytes 12292
  39.1 1.7 %collective-permute-start.6 = (f32[48,128]{1,0:T(8,128)S(1)}, f32[48,128]{1,0:T(8,128)S(1)}, u32[]{:S(2)}, u32[]{:S(2)}) collective-permute-start(f32[48,128]{1,0:T(8,128)S(1)} %forward.1), channel_id=1, source_target_pairs={{0,1},{1,0},{2,3},{3,2},{4,5},{5,4},{6,7},{7,6},{8,9},{9,8},{10,11... | collective-permute-start | bytes 73736 | tf_op jit(solution)/shard_map/ppermute | solution.py:23
  40.8 4.2 %collective-permute-start.7 = (f32[48,128]{1,0:T(8,128)S(1)}, f32[48,128]{1,0:T(8,128)S(1)}, u32[]{:S(2)}, u32[]{:S(2)}) collective-permute-start(f32[48,128]{1,0:T(8,128)S(1)} %add.50), channel_id=1, source_target_pairs={{0,2},{1,3},{2,0},{3,1},{4,6},{5,7},{6,4},{7,5},{8,10},{9,11},{10,... | collective-permute-start | bytes 73736 | tf_op jit(solution)/shard_map/ppermute | solution.py:23

commit v5 on v4

--- a/solution.py
+++ b/solution.py
@@ -5,9 +5,8 @@
 from jax.experimental.pallas import tpu as pltpu
 from jax.sharding import PartitionSpec as P
 
-Y_LO, X_HIGH, X_LOW, Y_HI, CORE = 128, 64, 32, 2, 1
-MIRROR = X_HIGH + X_LOW
-QUARTER_BITS = Y_LO + MIRROR
+Y_LO, X_LOW, Y_HI, CORE = 128, 32, 2, 1
+MIRROR = 64 + 32
 DEVICES = 256
 BLOCKS, SLOTS, COMPONENTS, STATES, HALF = 4, 5, 6, 256, 128
 PAIRS = BLOCKS * SLOTS
@@ -16,21 +15,12 @@
 FIRST_PHONON = 192
 ROWS = BLOCKS * COMPONENTS
 OWNERS = PHONON // BLOCKS
-QUARTERS = [[quarter * OWNERS + owner for owner in range(OWNERS)] for quarter in range(4)]
+LINE = 8
+SAME_X = [[y * 4 * LINE + x * LINE + z for y in range(2) for z in range(LINE)] for x in range(4)]
 
 
 def swap(value, bit):
     return lax.ppermute(value, ("grp", "rep"), [(i, i ^ bit) for i in range(DEVICES)])
-
-
-def from_phonon(value, bits):
-    pairs = [(i, i ^ bits) for i in range(DEVICES) if i & QUARTER_BITS == QUARTER_BITS]
-    return lax.ppermute(value, ("grp", "rep"), pairs)
-
-
-def to_phonon(value, bits):
-    pairs = [(i ^ bits, i) for i in range(DEVICES) if i & QUARTER_BITS == QUARTER_BITS]
-    return lax.ppermute(value, ("grp", "rep"), pairs)
 
 
 def split(value):
@@ -260,9 +250,12 @@
 
 
 def on_device(deviation, source, lifetime, rates, partner, count):
+    grp = lax.axis_index("grp")
     core = lax.axis_index("rep") % 2
-    quarter = lax.axis_index("grp") // OWNERS
-    is_phonon = quarter == 3
+    x = grp // LINE % 4
+    x_high = x >= 2
+    outer = (x == 0) | (x == 3)
+    is_phonon = x_high & (grp >= 2 * OWNERS)
     live = count.T
     turned = deviation.transpose(1, 0, 2)
 
@@ -271,21 +264,24 @@
 
     keep, give = spread(live, partner, turned, rates)
     drag = (keep + swap(give, CORE)).reshape(OWNERS, ROWS, HALF)
-    half = OWNERS // 2
-    drag = jnp.where(quarter % 2 == 1, drag, jnp.concatenate([drag[half:], drag[:half]]))
-
+
+    drag = jnp.where(outer, drag, jnp.concatenate([drag[LINE:], drag[:LINE]]))
     parcel = jnp.where(is_phonon, own, drag)
-    arrived = lax.all_to_all(parcel, "grp", 0, 0, axis_index_groups=QUARTERS, tiled=True)
+    arrived = lax.all_to_all(parcel, "grp", 0, 0, axis_index_groups=SAME_X, tiled=True)
     arrived, live = lax.optimization_barrier((arrived, live))
     rates_high, rates_low, token = prepare(live, partner, rates)
-    drag = arrived.sum(0)
-    gathered = arrived.reshape(PHONON * COMPONENTS, HALF)
-    spare = jnp.zeros((PHONON * COMPONENTS - ROWS, HALF), jnp.float32)
-    outgoing = jnp.where(is_phonon, gathered, jnp.concatenate([drag, spare]))
-    incoming = [swap(outgoing, bits) for bits in (QUARTER_BITS, MIRROR, Y_LO)]
-    drag = incoming[0][:ROWS] + incoming[1][:ROWS] + incoming[2][:ROWS]
-    phonon = jnp.where(quarter == 0, incoming[0], jnp.where(quarter == 1, incoming[2], incoming[1]))
-    phonon = jnp.where(is_phonon, gathered, phonon)
+    drag = arrived[:LINE].sum(0) + jnp.where(x_high, 0.0, arrived[LINE:].sum(0))
+    line = arrived[LINE:].reshape(LINE * ROWS, HALF)
+
+    spare = jnp.zeros((LINE * ROWS - ROWS, HALF), jnp.float32)
+    incoming = swap(jnp.where(x_high, line, jnp.concatenate([drag, spare])), MIRROR)
+    line = jnp.where(x_high, line, incoming)
+    drag = drag + incoming[:ROWS]
+
+    other = swap(line, X_LOW)
+    drag = drag + swap(drag, X_LOW + Y_LO)
+    first, second = jnp.where(outer, other, line), jnp.where(outer, line, other)
+    phonon = jnp.concatenate([first, second])
     phonon, token = lax.optimization_barrier((phonon, swap(token, CORE)))
     drag = jnp.where(is_phonon, drag + token[:1], 0.0)
     total = forward(live, partner, phonon, swap(phonon, CORE), rates_high, rates_low, drag)

time: 46.2 us -> 44.8 us (0.970)
  starting transfers between devices: 17.6 us -> 15.4 us
  Pallas kernels: 6.47 us -> 7.31 us
    ppermute x8, starting transfers between devices: 17.6 us -> 15.4 us  [swap(): lax.ppermute(value, ('grp', 'rep'), [(i, i ^ bit) for i in range(DEVICES)])]
  transfers between devices with their start and end apart: 8 -> 8, of which waited for: 5 -> 5; matrix products, arithmetic and copies ran while one was open for 0% -> 0% of each run, Pallas kernels for 5% -> 6%
where the time goes in v5:
time: 44.8 us; the launch traced here: 44.4 us
  starting transfers between devices  15.4 us (34%)
  blocking collectives  14.8 us (33%)
  Pallas kernels  7.31 us (16%)
  waiting for transfers between devices  5.83 us (13%)
  local copies, waits for them, and re-layouts  0.69 us (2%)
    ppermute x8, starting transfers between devices, swap(): lax.ppermute(value, ('grp', 'rep'), [(i, i ^ bit) for i in range(DEVICES)])  15.4 us
    all_to_all x1, blocking collectives, on_device(): lax.all_to_all(parcel, 'grp', 0, 0, axis_index_groups=SAME_X, tiled=True)  14.8 us
    ppermute x8, waiting for transfers between devices, swap(): lax.ppermute(value, ('grp', 'rep'), [(i, i ^ bit) for i in range(DEVICES)])  5.83 us
    pallas_call x1, Pallas kernels, spread(): rate_kernel(spread_kernel, 'spread', [float_rows(PHONON * COMPONENTS)] *...  2.84 us
    pallas_call x1, Pallas kernels, prepare(): rate_kernel(prepare_kernel, 'prepare', terms + [float_rows(8)], [HBM] * 3...  2.61 us
    pallas_call x1, Pallas kernels, forward(): rate_kernel(forward_kernel, 'forward', [float_rows(2 * ROWS)], [pl.BlockS...  1.86 us
  transfers between devices with their start and end apart: 8, of which 5 were waited for; matrix products, arithmetic and copies ran while one was open for 0% of the time, Pallas kernels for 6%

profile of v5, /device:TPU:1, one launch (start us, length us, event | category | flops | bytes accessed | tf_op | source)
XLA Modules:
  0.0 44.4 jit_solution(9357478788470810431)
XLA Ops:
  0.0 0.0 copy-start.2
  0.0 2.8 %spread.1 = (f32[384,128]{1,0:T(8,128)S(1)}, f32[384,128]{1,0:T(8,128)S(1)}) custom-call(s32[1,4]{1,0:T(1,128)} %bitcast.10, s32[4,5]{1,0:T(4,128)} %partner_hbm.5, f32[6,4,256]{2,1,0:T(4,128)} %bitcast.16, f32[4,5,256,256]{3,2,1,0:T(8,128)} %rates.3), custom_call_target="tpu_custom_call" | custom-call | flops 62914560 | bytes 10485760 | tf_op jit(solution)/shard_map/spread/pallas_call | solution.py:228
  2.8 3.4 %collective-permute-start = (f32[384,128]{1,0:T(8,128)S(1)}, f32[384,128]{1,0:T(8,128)S(1)}, u32[]{:S(2)}, u32[]{:S(2)}) collective-permute-start(f32[384,128]{1,0:T(8,128)S(1)} %get-tuple-element.15), channel_id=1, source_target_pairs={{0,1},{1,0},{2,3},{3,2},{4,5},{5,4},{6,7},{7,6},{8,9},{9,8},{10,11... | collective-permute-start | bytes 589832 | tf_op jit(solution)/shard_map/ppermute | solution.py:23
  6.2 0.0 copy-done.2
  6.3 1.0 %collective-permute-done = f32[384,128]{1,0:T(8,128)S(1)} collective-permute-done((f32[384,128]{1,0:T(8,128)S(1)}, f32[384,128]{1,0:T(8,128)S(1)}, u32[]{:S(2)}, u32[]{:S(2)}) %collective-permute-start) | collective-permute-done | bytes 196640 | tf_op jit(solution)/shard_map/ppermute | solution.py:23
  7.4 14.8 %all_to_all.5 = f32[16,24,128]{2,1,0:T(8,128)S(1)} all-to-all(f32[16,24,128]{2,1,0:T(8,128)S(1)} %fusion), channel_id=1, replica_groups={{0,4,8,12,16,20,24,28,128,132,136,140,144,148,152,156},{32,36,40,44,48,..., dimensions={0} | all-to-all | bytes 393216 | tf_op jit(solution)/shard_map/all_to_all | solution.py:270
  22.3 0.0 copy-start
  22.3 0.0 copy-start.1
  22.3 1.6 %collective-permute-start.1 = (f32[192,128]{1,0:T(8,128)S(1)}, f32[192,128]{1,0:T(8,128)S(1)}, u32[]{:S(2)}, u32[]{:S(2)}) collective-permute-start(f32[192,128]{1,0:T(8,128)S(1)} %bitcast_select_fusion.1), channel_id=1, source_target_pairs={{0,96},{1,97},{2,98},{3,99},{4,100},{5,101},{6,102},{7,103},{8,104... | collective-permute-start | bytes 294920 | tf_op jit(solution)/shard_map/ppermute | solution.py:23
  23.9 2.6 %prepare.1 = (bf16[20,256,256]{2,1,0:T(8,128)(2,1)S(1)}, bf16[20,256,256]{2,1,0:T(8,128)(2,1)S(1)}, f32[8,128]{1,0:T(8,128)S(1)}) custom-call(s32[1,4]{1,0:T(1,128)} %bitcast.11, s32[4,5]{1,0:T(4,128)} %partner_hbm.5, f32[4,5,256,256]{3,2,1,0:T(8,128)} %rates.3), custom_call_target="tpu_custom_call" | custom-call | flops 62914560 | bytes 10485760 | tf_op jit(solution)/shard_map/prepare/pallas_call | solution.py:236
  26.5 2.7 %collective-permute-start.3 = (f32[8,128]{1,0:T(8,128)S(1)}, f32[8,128]{1,0:T(8,128)S(1)}, u32[]{:S(2)}, u32[]{:S(2)}) collective-permute-start(f32[8,128]{1,0:T(8,128)S(1)} %get-tuple-element.18), channel_id=1, source_target_pairs={{0,1},{1,0},{2,3},{3,2},{4,5},{5,4},{6,7},{7,6},{8,9},{9,8},{10,11... | collective-permute-start | bytes 12296 | tf_op jit(solution)/shard_map/ppermute | solution.py:23
  29.2 0.0 collective-permute-done.1
  29.2 0.1 collective-permute-start.2
  29.3 2.1 %collective-permute-start.5 = (f32[24,128]{1,0:T(8,128)S(1)}, f32[24,128]{1,0:T(8,128)S(1)}, u32[]{:S(2)}, u32[]{:S(2)}) collective-permute-start(f32[24,128]{1,0:T(8,128)S(1)} %slice_add_fusion), channel_id=1, source_target_pairs={{0,160},{1,161},{2,162},{3,163},{4,164},{5,165},{6,166},{7,167},{8... | collective-permute-start | bytes 36872 | tf_op jit(solution)/shard_map/ppermute | solution.py:23
  31.4 1.4 %collective-permute-done.2 = f32[192,128]{1,0:T(8,128)S(1)} collective-permute-done((f32[192,128]{1,0:T(8,128)S(1)}, f32[192,128]{1,0:T(8,128)S(1)}, u32[]{:S(2)}, u32[]{:S(2)}) %collective-permute-start.2) | collective-permute-done | bytes 98336 | tf_op jit(solution)/shard_map/ppermute | solution.py:23
  32.8 0.0 collective-permute-done.3
  32.8 2.5 %collective-permute-start.4 = (f32[384,128]{1,0:T(8,128)S(1)}, f32[384,128]{1,0:T(8,128)S(1)}, u32[]{:S(2)}, u32[]{:S(2)}) collective-permute-start(f32[384,128]{1,0:T(8,128)S(1)} %pad_maximum_fusion.mine), channel_id=1, source_target_pairs={{0,1},{1,0},{2,3},{3,2},{4,5},{5,4},{6,7},{7,6},{8,9},{9,8},{10,11... | collective-permute-start | bytes 589832 | tf_op jit(solution)/shard_map/ppermute | solution.py:23
  35.3 0.0 collective-permute-done.5
  35.3 1.1 %collective-permute-done.4.other = f32[384,128]{1,0:T(8,128)S(1)} collective-permute-done((f32[384,128]{1,0:T(8,128)S(1)}, f32[384,128]{1,0:T(8,128)S(1)}, u32[]{:S(2)}, u32[]{:S(2)}) %collective-permute-start.4) | collective-permute-done | bytes 196640 | tf_op jit(solution)/shard_map/ppermute | solution.py:23
  36.3 0.0 copy-done
  36.3 0.0 copy-done.1
  36.3 0.0 copy-start.3
  36.3 0.0 copy-start.4
  36.4 1.9 %forward.1 = f32[48,128]{1,0:T(8,128)S(1)} custom-call(s32[1,4]{1,0:T(1,128)S(1)} %bitcast.12, s32[4,5]{1,0:T(4,128)S(1)} %copy-done, f32[384,128]{1,0:T(8,128)S(1)} %pad_maximum_fusion.mine, f32[384,128]{1,0:T(8,128)S(1)} %collective-permute-done.4.other, bf16[20,256,256]{2,1,0:T(8,128)(2,1)S(1)} %get-tuple-element.20.high_ref, ...), custom_call_target="tpu_custom_call" | custom-call | flops 62914560 | bytes 10485760 | tf_op jit(solution)/shard_map/forward/pallas_call | solution.py:243
  38.2 0.5 %collective-permute-start.6 = (f32[48,128]{1,0:T(8,128)S(1)}, f32[48,128]{1,0:T(8,128)S(1)}, u32[]{:S(2)}, u32[]{:S(2)}) collective-permute-start(f32[48,128]{1,0:T(8,128)S(1)} %forward.1), channel_id=1, source_target_pairs={{0,1},{1,0},{2,3},{3,2},{4,5},{5,4},{6,7},{7,6},{8,9},{9,8},{10,11... | collective-permute-start | bytes 73736 | tf_op jit(solution)/shard_map/ppermute | solution.py:23
  38.7 0.8 %collective-permute-done.6 = f32[48,128]{1,0:T(8,128)S(1)} collective-permute-done((f32[48,128]{1,0:T(8,128)S(1)}, f32[48,128]{1,0:T(8,128)S(1)}, u32[]{:S(2)}, u32[]{:S(2)}) %collective-permute-start.6) | collective-permute-done | bytes 24608 | tf_op jit(solution)/shard_map/ppermute | solution.py:23
  39.6 2.7 %collective-permute-start.7 = (f32[48,128]{1,0:T(8,128)S(1)}, f32[48,128]{1,0:T(8,128)S(1)}, u32[]{:S(2)}, u32[]{:S(2)}) collective-permute-start(f32[48,128]{1,0:T(8,128)S(1)} %add.54), channel_id=1, source_target_pairs={{0,2},{1,3},{2,0},{3,1},{4,6},{5,7},{6,4},{7,5},{8,10},{9,11},{10,... | collective-permute-start | bytes 73736 | tf_op jit(solution)/shard_map/ppermute | solution.py:23
  42.2 1.5 %collective-permute-done.7 = f32[48,128]{1,0:T(8,128)S(1)} collective-permute-done((f32[48,128]{1,0:T(8,128)S(1)}, f32[48,128]{1,0:T(8,128)S(1)}, u32[]{:S(2)}, u32[]{:S(2)}) %collective-permute-start.7) | collective-permute-done | bytes 24608 | tf_op jit(solution)/shard_map/ppermute | solution.py:23
  43.8 0.0 copy-done.3
  43.8 0.0 copy-done.4
  43.8 0.6 %copy.11 = f32[4,6,256]{2,0,1:T(4,128)} copy(f32[4,6,256]{2,1,0:T(8,128)S(1)} %fusion.1) | data formatting | bytes 49152 | tf_op jit(solution)/shard_map/add | solution.py:292
  (21 shorter events, 0.2 us)
Async XLA Ops:
  0.0 6.2 %copy-start.2 = (f32[4,6,256]{2,0,1:T(4,128)S(1)}, f32[4,6,256]{2,0,1:T(4,128)}, u32[]{:S(2)}) copy-start(f32[4,6,256]{2,0,1:T(4,128)} %param.6) | copy-start | bytes 73732
  2.8 4.5 %collective-permute-start = (f32[384,128]{1,0:T(8,128)S(1)}, f32[384,128]{1,0:T(8,128)S(1)}, u32[]{:S(2)}, u32[]{:S(2)}) collective-permute-start(f32[384,128]{1,0:T(8,128)S(1)} %get-tuple-element.15), channel_id=1, source_target_pairs={{0,1},{1,0},{2,3},{3,2},{4,5},{5,4},{6,7},{7,6},{8,9},{9,8},{10,11... | collective-permute-start | bytes 589832 | tf_op jit(solution)/shard_map/ppermute | solution.py:23
  22.3 14.1 %copy-start = (s32[4,5]{1,0:T(4,128)S(1)}, s32[4,5]{1,0:T(4,128)}, u32[]{:S(2)}) copy-start(s32[4,5]{1,0:T(4,128)} %partner_hbm.5) | copy-start | bytes 244
  22.3 14.0 %copy-start.1 = (s32[4,1]{0,1:T(1,128)S(1)}, s32[4,1]{0,1:T(1,128)}, u32[]{:S(2)}) copy-start(s32[4,1]{0,1:T(1,128)} %param.11) | copy-start | bytes 52
  22.3 6.8 %collective-permute-start.1 = (f32[192,128]{1,0:T(8,128)S(1)}, f32[192,128]{1,0:T(8,128)S(1)}, u32[]{:S(2)}, u32[]{:S(2)}) collective-permute-start(f32[192,128]{1,0:T(8,128)S(1)} %bitcast_select_fusion.1), channel_id=1, source_target_pairs={{0,96},{1,97},{2,98},{3,99},{4,100},{5,101},{6,102},{7,103},{8,104... | collective-permute-start | bytes 294920 | tf_op jit(solution)/shard_map/ppermute | solution.py:23
  26.5 6.3 %collective-permute-start.3 = (f32[8,128]{1,0:T(8,128)S(1)}, f32[8,128]{1,0:T(8,128)S(1)}, u32[]{:S(2)}, u32[]{:S(2)}) collective-permute-start(f32[8,128]{1,0:T(8,128)S(1)} %get-tuple-element.18), channel_id=1, source_target_pairs={{0,1},{1,0},{2,3},{3,2},{4,5},{5,4},{6,7},{7,6},{8,9},{9,8},{10,11... | collective-permute-start | bytes 12296 | tf_op jit(solution)/shard_map/ppermute | solution.py:23
  29.2 3.6 %collective-permute-start.2 = (f32[192,128]{1,0:T(8,128)S(1)}, f32[192,128]{1,0:T(8,128)S(1)}, u32[]{:S(2)}, u32[]{:S(2)}) collective-permute-start(f32[192,128]{1,0:T(8,128)S(1)} %bitcast_select_fusion), channel_id=1, source_target_pairs={{0,32},{1,33},{2,34},{3,35},{4,36},{5,37},{6,38},{7,39},{8,40},{9,... | collective-permute-start | bytes 294920 | tf_op jit(solution)/shard_map/ppermute | solution.py:23
  29.3 6.0 %collective-permute-start.5 = (f32[24,128]{1,0:T(8,128)S(1)}, f32[24,128]{1,0:T(8,128)S(1)}, u32[]{:S(2)}, u32[]{:S(2)}) collective-permute-start(f32[24,128]{1,0:T(8,128)S(1)} %slice_add_fusion), channel_id=1, source_target_pairs={{0,160},{1,161},{2,162},{3,163},{4,164},{5,165},{6,166},{7,167},{8... | collective-permute-start | bytes 36872 | tf_op jit(solution)/shard_map/ppermute | solution.py:23
  32.8 3.5 %collective-permute-start.4 = (f32[384,128]{1,0:T(8,128)S(1)}, f32[384,128]{1,0:T(8,128)S(1)}, u32[]{:S(2)}, u32[]{:S(2)}) collective-permute-start(f32[384,128]{1,0:T(8,128)S(1)} %pad_maximum_fusion.mine), channel_id=1, source_target_pairs={{0,1},{1,0},{2,3},{3,2},{4,5},{5,4},{6,7},{7,6},{8,9},{9,8},{10,11... | collective-permute-start | bytes 589832 | tf_op jit(solution)/shard_map/ppermute | solution.py:23
  36.3 7.4 %copy-start.3 = (f32[4,6,256]{2,0,1:T(4,128)S(1)}, f32[4,6,256]{2,0,1:T(4,128)}, u32[]{:S(2)}) copy-start(f32[4,6,256]{2,0,1:T(4,128)} %param.7) | copy-start | bytes 73732
  36.3 7.4 %copy-start.4 = (f32[4,256]{1,0:T(4,128)S(1)}, f32[4,256]{1,0:T(4,128)}, u32[]{:S(2)}) copy-start(f32[4,256]{1,0:T(4,128)} %param.8) | copy-start | bytes 12292
  38.2 1.3 %collective-permute-start.6 = (f32[48,128]{1,0:T(8,128)S(1)}, f32[48,128]{1,0:T(8,128)S(1)}, u32[]{:S(2)}, u32[]{:S(2)}) collective-permute-start(f32[48,128]{1,0:T(8,128)S(1)} %forward.1), channel_id=1, source_target_pairs={{0,1},{1,0},{2,3},{3,2},{4,5},{5,4},{6,7},{7,6},{8,9},{9,8},{10,11... | collective-permute-start | bytes 73736 | tf_op jit(solution)/shard_map/ppermute | solution.py:23
  39.6 4.2 %collective-permute-start.7 = (f32[48,128]{1,0:T(8,128)S(1)}, f32[48,128]{1,0:T(8,128)S(1)}, u32[]{:S(2)}, u32[]{:S(2)}) collective-permute-start(f32[48,128]{1,0:T(8,128)S(1)} %add.54), channel_id=1, source_target_pairs={{0,2},{1,3},{2,0},{3,1},{4,6},{5,7},{6,4},{7,5},{8,10},{9,11},{10,... | collective-permute-start | bytes 73736 | tf_op jit(solution)/shard_map/ppermute | solution.py:23

commit v6 on v5

--- a/solution.py
+++ b/solution.py
@@ -70,14 +70,16 @@
 
 
 def visit_live(count, chosen, fetch, visit):
-    total = jnp.int32(0)
+    for block in range(BLOCKS):
+        chosen[block] = block * SLOTS
+    total = jnp.int32(BLOCKS)
     for block in range(BLOCKS):
 
         def note(slot, at):
             chosen[at] = block * SLOTS + slot
             return at + 1
 
-        total = lax.fori_loop(0, count[0, block], note, total)
+        total = lax.fori_loop(1, count[0, block], note, total)
 
     @pl.loop(0, lax.div(total + (UNROLL - 1), UNROLL))
     def _(step):
@@ -287,9 +289,10 @@
     total = forward(live, partner, phonon, swap(phonon, CORE), rates_high, rates_low, drag)
     total = total + swap(total, CORE)
     total = total + swap(total, Y_HI)
-    total = total.reshape(2, BLOCKS, COMPONENTS, HALF)
+    total = total.reshape(2, BLOCKS, COMPONENTS, HALF).transpose(0, 2, 1, 3)
     summed = jnp.concatenate([total[0], total[1]], axis=-1)
-    return source + lifetime[:, None, :] * summed
+    result = source.transpose(1, 0, 2) + lifetime[None] * summed
+    return result.transpose(1, 0, 2)
 
 
 def solution(mesh):

time: 44.8 us -> 44.7 us (level)
  starting transfers between devices: 15.4 us -> 13.7 us
  waiting for transfers between devices: 5.83 us -> 6.83 us
  Pallas kernels: 7.31 us -> 8.29 us
    ppermute x8, starting transfers between devices: 15.4 us -> 13.7 us  [swap(): lax.ppermute(value, ('grp', 'rep'), [(i, i ^ bit) for i in range(DEVICES)])]
    ppermute x8, waiting for transfers between devices: 5.83 us -> 6.83 us  [swap(): lax.ppermute(value, ('grp', 'rep'), [(i, i ^ bit) for i in range(DEVICES)])]
    add x1 -> x0, local copies, waits for them, and re-layouts: 0.62 us -> none  [on_device(): return source + lifetime[:, None, :] * summed]
    transpose x0 -> x1, local copies, waits for them, and re-layouts: none -> 0.62 us  [on_device(): return result.transpose(1, 0, 2)]
  transfers between devices with their start and end apart: 8 -> 8, of which waited for: 5 -> 5; matrix products, arithmetic and copies ran while one was open for 0% -> 0% of each run, Pallas kernels for 6% -> 7%
where the time goes in v6:
time: 44.7 us
  blocking collectives  14.8 us (33%)
  starting transfers between devices  13.7 us (31%)
  Pallas kernels  8.29 us (19%)
  waiting for transfers between devices  6.83 us (15%)
  local copies, waits for them, and re-layouts  0.69 us (2%)
    all_to_all x1, blocking collectives, on_device(): lax.all_to_all(parcel, 'grp', 0, 0, axis_index_groups=SAME_X, tiled=True)  14.8 us
    ppermute x8, starting transfers between devices, swap(): lax.ppermute(value, ('grp', 'rep'), [(i, i ^ bit) for i in range(DEVICES)])  13.7 us
    ppermute x8, waiting for transfers between devices, swap(): lax.ppermute(value, ('grp', 'rep'), [(i, i ^ bit) for i in range(DEVICES)])  6.83 us
    pallas_call x1, Pallas kernels, spread(): rate_kernel(spread_kernel, 'spread', [float_rows(PHONON * COMPONENTS)] *...  3.11 us
    pallas_call x1, Pallas kernels, prepare(): rate_kernel(prepare_kernel, 'prepare', terms + [float_rows(8)], [HBM] * 3...  2.91 us
    pallas_call x1, Pallas kernels, forward(): rate_kernel(forward_kernel, 'forward', [float_rows(2 * ROWS)], [pl.BlockS...  2.26 us
  transfers between devices with their start and end apart: 8, of which 5 were waited for; matrix products, arithmetic and copies ran while one was open for 0% of the time, Pallas kernels for 7%

profile of v6, /device:TPU:1, one launch (start us, length us, event | category | flops | bytes accessed | tf_op | source)
XLA Modules:
  0.0 44.7 jit_solution(2131435729999904315)
XLA Ops:
  0.0 0.0 copy-start.2
  0.0 3.1 %spread.1 = (f32[384,128]{1,0:T(8,128)S(1)}, f32[384,128]{1,0:T(8,128)S(1)}) custom-call(s32[1,4]{1,0:T(1,128)} %bitcast.19, s32[4,5]{1,0:T(4,128)} %partner_hbm.5, f32[6,4,256]{2,1,0:T(4,128)} %bitcast.26, f32[4,5,256,256]{3,2,1,0:T(8,128)} %rates.3), custom_call_target="tpu_custom_call" | custom-call | flops 62914560 | bytes 10485760 | tf_op jit(solution)/shard_map/spread/pallas_call | solution.py:230
  3.1 3.0 %collective-permute-start = (f32[384,128]{1,0:T(8,128)S(1)}, f32[384,128]{1,0:T(8,128)S(1)}, u32[]{:S(2)}, u32[]{:S(2)}) collective-permute-start(f32[384,128]{1,0:T(8,128)S(1)} %get-tuple-element.15), channel_id=1, source_target_pairs={{0,1},{1,0},{2,3},{3,2},{4,5},{5,4},{6,7},{7,6},{8,9},{9,8},{10,11... | collective-permute-start | bytes 589832 | tf_op jit(solution)/shard_map/ppermute | solution.py:23
  6.1 0.0 copy-done.2
  6.2 1.0 %collective-permute-done = f32[384,128]{1,0:T(8,128)S(1)} collective-permute-done((f32[384,128]{1,0:T(8,128)S(1)}, f32[384,128]{1,0:T(8,128)S(1)}, u32[]{:S(2)}, u32[]{:S(2)}) %collective-permute-start) | collective-permute-done | bytes 196640 | tf_op jit(solution)/shard_map/ppermute | solution.py:23
  7.3 14.8 %all_to_all.5 = f32[16,24,128]{2,1,0:T(8,128)S(1)} all-to-all(f32[16,24,128]{2,1,0:T(8,128)S(1)} %fusion), channel_id=1, replica_groups={{0,4,8,12,16,20,24,28,128,132,136,140,144,148,152,156},{32,36,40,44,48,..., dimensions={0} | all-to-all | bytes 393216 | tf_op jit(solution)/shard_map/all_to_all | solution.py:272
  22.2 0.0 copy-start
  22.2 0.0 copy-start.1
  22.2 1.4 %collective-permute-start.1 = (f32[192,128]{1,0:T(8,128)S(1)}, f32[192,128]{1,0:T(8,128)S(1)}, u32[]{:S(2)}, u32[]{:S(2)}) collective-permute-start(f32[192,128]{1,0:T(8,128)S(1)} %bitcast_select_fusion.1), channel_id=1, source_target_pairs={{0,96},{1,97},{2,98},{3,99},{4,100},{5,101},{6,102},{7,103},{8,104... | collective-permute-start | bytes 294920 | tf_op jit(solution)/shard_map/ppermute | solution.py:23
  23.6 2.9 %prepare.1 = (bf16[20,256,256]{2,1,0:T(8,128)(2,1)S(1)}, bf16[20,256,256]{2,1,0:T(8,128)(2,1)S(1)}, f32[8,128]{1,0:T(8,128)S(1)}) custom-call(s32[1,4]{1,0:T(1,128)} %bitcast.20, s32[4,5]{1,0:T(4,128)} %partner_hbm.5, f32[4,5,256,256]{3,2,1,0:T(8,128)} %rates.3), custom_call_target="tpu_custom_call" | custom-call | flops 62914560 | bytes 10485760 | tf_op jit(solution)/shard_map/prepare/pallas_call | solution.py:238
  26.5 2.2 %collective-permute-start.3 = (f32[8,128]{1,0:T(8,128)S(1)}, f32[8,128]{1,0:T(8,128)S(1)}, u32[]{:S(2)}, u32[]{:S(2)}) collective-permute-start(f32[8,128]{1,0:T(8,128)S(1)} %get-tuple-element.18), channel_id=1, source_target_pairs={{0,1},{1,0},{2,3},{3,2},{4,5},{5,4},{6,7},{7,6},{8,9},{9,8},{10,11... | collective-permute-start | bytes 12296 | tf_op jit(solution)/shard_map/ppermute | solution.py:23
  28.8 0.0 collective-permute-done.1
  28.8 0.1 collective-permute-start.2
  28.9 2.0 %collective-permute-start.5 = (f32[24,128]{1,0:T(8,128)S(1)}, f32[24,128]{1,0:T(8,128)S(1)}, u32[]{:S(2)}, u32[]{:S(2)}) collective-permute-start(f32[24,128]{1,0:T(8,128)S(1)} %slice_add_fusion), channel_id=1, source_target_pairs={{0,160},{1,161},{2,162},{3,163},{4,164},{5,165},{6,166},{7,167},{8... | collective-permute-start | bytes 36872 | tf_op jit(solution)/shard_map/ppermute | solution.py:23
  30.9 1.5 %collective-permute-done.2 = f32[192,128]{1,0:T(8,128)S(1)} collective-permute-done((f32[192,128]{1,0:T(8,128)S(1)}, f32[192,128]{1,0:T(8,128)S(1)}, u32[]{:S(2)}, u32[]{:S(2)}) %collective-permute-start.2) | collective-permute-done | bytes 98336 | tf_op jit(solution)/shard_map/ppermute | solution.py:23
  32.4 0.0 collective-permute-done.3
  32.4 2.7 %collective-permute-start.4 = (f32[384,128]{1,0:T(8,128)S(1)}, f32[384,128]{1,0:T(8,128)S(1)}, u32[]{:S(2)}, u32[]{:S(2)}) collective-permute-start(f32[384,128]{1,0:T(8,128)S(1)} %pad_maximum_fusion.mine), channel_id=1, source_target_pairs={{0,1},{1,0},{2,3},{3,2},{4,5},{5,4},{6,7},{7,6},{8,9},{9,8},{10,11... | collective-permute-start | bytes 589832 | tf_op jit(solution)/shard_map/ppermute | solution.py:23
  35.2 0.0 collective-permute-done.5
  35.2 1.1 %collective-permute-done.4.other = f32[384,128]{1,0:T(8,128)S(1)} collective-permute-done((f32[384,128]{1,0:T(8,128)S(1)}, f32[384,128]{1,0:T(8,128)S(1)}, u32[]{:S(2)}, u32[]{:S(2)}) %collective-permute-start.4) | collective-permute-done | bytes 196640 | tf_op jit(solution)/shard_map/ppermute | solution.py:23
  36.2 0.0 copy-done
  36.2 0.0 copy-done.1
  36.2 0.0 copy-start.3
  36.2 0.0 copy-start.4
  36.2 2.3 %forward.1 = f32[48,128]{1,0:T(8,128)S(1)} custom-call(s32[1,4]{1,0:T(1,128)S(1)} %bitcast.21, s32[4,5]{1,0:T(4,128)S(1)} %copy-done, f32[384,128]{1,0:T(8,128)S(1)} %pad_maximum_fusion.mine, f32[384,128]{1,0:T(8,128)S(1)} %collective-permute-done.4.other, bf16[20,256,256]{2,1,0:T(8,128)(2,1)S(1)} %get-tuple-element.20.high_ref, ...), custom_call_target="tpu_custom_call" | custom-call | flops 62914560 | bytes 10485760 | tf_op jit(solution)/shard_map/forward/pallas_call | solution.py:245
  38.5 0.1 collective-permute-start.6
  38.6 1.2 %collective-permute-done.6 = f32[48,128]{1,0:T(8,128)S(1)} collective-permute-done((f32[48,128]{1,0:T(8,128)S(1)}, f32[48,128]{1,0:T(8,128)S(1)}, u32[]{:S(2)}, u32[]{:S(2)}) %collective-permute-start.6) | collective-permute-done | bytes 24608 | tf_op jit(solution)/shard_map/ppermute | solution.py:23
  39.8 2.1 %collective-permute-start.7 = (f32[48,128]{1,0:T(8,128)S(1)}, f32[48,128]{1,0:T(8,128)S(1)}, u32[]{:S(2)}, u32[]{:S(2)}) collective-permute-start(f32[48,128]{1,0:T(8,128)S(1)} %add.54), channel_id=1, source_target_pairs={{0,2},{1,3},{2,0},{3,1},{4,6},{5,7},{6,4},{7,5},{8,10},{9,11},{10,... | collective-permute-start | bytes 73736 | tf_op jit(solution)/shard_map/ppermute | solution.py:23
  41.9 2.1 %collective-permute-done.7 = f32[48,128]{1,0:T(8,128)S(1)} collective-permute-done((f32[48,128]{1,0:T(8,128)S(1)}, f32[48,128]{1,0:T(8,128)S(1)}, u32[]{:S(2)}, u32[]{:S(2)}) %collective-permute-start.7) | collective-permute-done | bytes 24608 | tf_op jit(solution)/shard_map/ppermute | solution.py:23
  44.0 0.0 copy-done.3
  44.0 0.0 copy-done.4
  44.0 0.6 %copy.10 = f32[4,6,256]{2,0,1:T(4,128)} copy(f32[4,6,256]{2,1,0:T(8,128)S(1)} %fusion.2) | data formatting | bytes 49152 | tf_op jit(solution)/shard_map/transpose | solution.py:295
  (20 shorter events, 0.2 us)
Async XLA Ops:
  0.0 6.1 %copy-start.2 = (f32[4,6,256]{2,0,1:T(4,128)S(1)}, f32[4,6,256]{2,0,1:T(4,128)}, u32[]{:S(2)}) copy-start(f32[4,6,256]{2,0,1:T(4,128)} %param.6) | copy-start | bytes 73732
  3.1 4.1 %collective-permute-start = (f32[384,128]{1,0:T(8,128)S(1)}, f32[384,128]{1,0:T(8,128)S(1)}, u32[]{:S(2)}, u32[]{:S(2)}) collective-permute-start(f32[384,128]{1,0:T(8,128)S(1)} %get-tuple-element.15), channel_id=1, source_target_pairs={{0,1},{1,0},{2,3},{3,2},{4,5},{5,4},{6,7},{7,6},{8,9},{9,8},{10,11... | collective-permute-start | bytes 589832 | tf_op jit(solution)/shard_map/ppermute | solution.py:23
  22.2 14.1 %copy-start = (s32[4,5]{1,0:T(4,128)S(1)}, s32[4,5]{1,0:T(4,128)}, u32[]{:S(2)}) copy-start(s32[4,5]{1,0:T(4,128)} %partner_hbm.5) | copy-start | bytes 244
  22.2 14.0 %copy-start.1 = (s32[4,1]{0,1:T(1,128)S(1)}, s32[4,1]{0,1:T(1,128)}, u32[]{:S(2)}) copy-start(s32[4,1]{0,1:T(1,128)} %param.11) | copy-start | bytes 52
  22.2 6.6 %collective-permute-start.1 = (f32[192,128]{1,0:T(8,128)S(1)}, f32[192,128]{1,0:T(8,128)S(1)}, u32[]{:S(2)}, u32[]{:S(2)}) collective-permute-start(f32[192,128]{1,0:T(8,128)S(1)} %bitcast_select_fusion.1), channel_id=1, source_target_pairs={{0,96},{1,97},{2,98},{3,99},{4,100},{5,101},{6,102},{7,103},{8,104... | collective-permute-start | bytes 294920 | tf_op jit(solution)/shard_map/ppermute | solution.py:23
  26.5 5.9 %collective-permute-start.3 = (f32[8,128]{1,0:T(8,128)S(1)}, f32[8,128]{1,0:T(8,128)S(1)}, u32[]{:S(2)}, u32[]{:S(2)}) collective-permute-start(f32[8,128]{1,0:T(8,128)S(1)} %get-tuple-element.18), channel_id=1, source_target_pairs={{0,1},{1,0},{2,3},{3,2},{4,5},{5,4},{6,7},{7,6},{8,9},{9,8},{10,11... | collective-permute-start | bytes 12296 | tf_op jit(solution)/shard_map/ppermute | solution.py:23
  28.8 3.6 %collective-permute-start.2 = (f32[192,128]{1,0:T(8,128)S(1)}, f32[192,128]{1,0:T(8,128)S(1)}, u32[]{:S(2)}, u32[]{:S(2)}) collective-permute-start(f32[192,128]{1,0:T(8,128)S(1)} %bitcast_select_fusion), channel_id=1, source_target_pairs={{0,32},{1,33},{2,34},{3,35},{4,36},{5,37},{6,38},{7,39},{8,40},{9,... | collective-permute-start | bytes 294920 | tf_op jit(solution)/shard_map/ppermute | solution.py:23
  28.9 6.2 %collective-permute-start.5 = (f32[24,128]{1,0:T(8,128)S(1)}, f32[24,128]{1,0:T(8,128)S(1)}, u32[]{:S(2)}, u32[]{:S(2)}) collective-permute-start(f32[24,128]{1,0:T(8,128)S(1)} %slice_add_fusion), channel_id=1, source_target_pairs={{0,160},{1,161},{2,162},{3,163},{4,164},{5,165},{6,166},{7,167},{8... | collective-permute-start | bytes 36872 | tf_op jit(solution)/shard_map/ppermute | solution.py:23
  32.4 3.8 %collective-permute-start.4 = (f32[384,128]{1,0:T(8,128)S(1)}, f32[384,128]{1,0:T(8,128)S(1)}, u32[]{:S(2)}, u32[]{:S(2)}) collective-permute-start(f32[384,128]{1,0:T(8,128)S(1)} %pad_maximum_fusion.mine), channel_id=1, source_target_pairs={{0,1},{1,0},{2,3},{3,2},{4,5},{5,4},{6,7},{7,6},{8,9},{9,8},{10,11... | collective-permute-start | bytes 589832 | tf_op jit(solution)/shard_map/ppermute | solution.py:23
  36.2 7.8 %copy-start.3 = (f32[4,6,256]{2,0,1:T(4,128)S(1)}, f32[4,6,256]{2,0,1:T(4,128)}, u32[]{:S(2)}) copy-start(f32[4,6,256]{2,0,1:T(4,128)} %param.7) | copy-start | bytes 73732
  36.2 7.8 %copy-start.4 = (f32[4,256]{1,0:T(4,128)S(1)}, f32[4,256]{1,0:T(4,128)}, u32[]{:S(2)}) copy-start(f32[4,256]{1,0:T(4,128)} %param.8) | copy-start | bytes 12292
  38.5 1.3 %collective-permute-start.6 = (f32[48,128]{1,0:T(8,128)S(1)}, f32[48,128]{1,0:T(8,128)S(1)}, u32[]{:S(2)}, u32[]{:S(2)}) collective-permute-start(f32[48,128]{1,0:T(8,128)S(1)} %forward.1), channel_id=1, source_target_pairs={{0,1},{1,0},{2,3},{3,2},{4,5},{5,4},{6,7},{7,6},{8,9},{9,8},{10,11... | collective-permute-start | bytes 73736 | tf_op jit(solution)/shard_map/ppermute | solution.py:23
  39.8 4.2 %collective-permute-start.7 = (f32[48,128]{1,0:T(8,128)S(1)}, f32[48,128]{1,0:T(8,128)S(1)}, u32[]{:S(2)}, u32[]{:S(2)}) collective-permute-start(f32[48,128]{1,0:T(8,128)S(1)} %add.54), channel_id=1, source_target_pairs={{0,2},{1,3},{2,0},{3,1},{4,6},{5,7},{6,4},{7,5},{8,10},{9,11},{10,... | collective-permute-start | bytes 73736 | tf_op jit(solution)/shard_map/ppermute | solution.py:23

commit v7 on v6

--- a/solution.py
+++ b/solution.py
@@ -46,7 +46,7 @@
     return multiply(high, both, *split(weights), contract)
 
 
-def rate_copies(count_hbm, partner_hbm, rates, count, partner, held, sems, small_sems, meanwhile):
+def rate_copies(count_hbm, partner_hbm, rates, count, partner, held, sems, small_sems, meanwhile, sure=1):
     def fetch(block, slot):
         pair = block * SLOTS + slot
         return pltpu.make_async_copy(rates.at[block, slot], held.at[pair], sems.at[pair])
@@ -55,13 +55,14 @@
     partners = pltpu.make_async_copy(partner_hbm, partner, small_sems.at[1])
     counts.start()
     partners.start()
-    for block in range(BLOCKS):
-        fetch(block, 0).start()
+    for slot in range(sure):
+        for block in range(BLOCKS):
+            fetch(block, slot).start()
     meanwhile()
     counts.wait()
     for block in range(BLOCKS):
 
-        @pl.loop(1, count[0, block])
+        @pl.loop(sure, count[0, block])
         def _(slot):
             fetch(block, slot).start()
 
@@ -116,7 +117,7 @@
         own_copy = pltpu.make_async_copy(deviation, own, own_sem)
         own_copy.start()
         fetch = rate_copies(
-            count_hbm, partner_hbm, rates, count, partner, held, sems, small, clear
+            count_hbm, partner_hbm, rates, count, partner, held, sems, small, clear, 2
         )
         own_copy.wait()
         for block in range(BLOCKS):
@@ -135,6 +136,11 @@
                 give[pl.ds(row, COMPONENTS), :] += jnp.where(core == 0, right, left)
 
         visit_live(count, chosen, fetch, visit)
+        for block in range(BLOCKS):
+
+            @pl.when(count[0, block] < 2)
+            def _():
+                fetch(block, 1).wait()
 
 
 def prepare_kernel(count_hbm, partner_hbm, rates, high, low, token, held, count, partner, chosen, sems, small):

time: 44.7 us -> 44.5 us (level)
  starting transfers between devices: 13.7 us -> 15 us
  Pallas kernels: 8.29 us -> 7.19 us
    ppermute x8, starting transfers between devices: 13.7 us -> 15 us  [swap(): lax.ppermute(value, ('grp', 'rep'), [(i, i ^ bit) for i in range(DEVICES)])]
  transfers between devices with their start and end apart: 8 -> 8, of which waited for: 5 -> 5; matrix products, arithmetic and copies ran while one was open for 0% -> 0% of each run, Pallas kernels for 7% -> 6%
where the time goes in v7:
time: 44.5 us; the launch traced here: 44.6 us
  starting transfers between devices  15 us (34%)
  blocking collectives  14.6 us (33%)
  Pallas kernels  7.19 us (16%)
  waiting for transfers between devices  6.87 us (15%)
  local copies, waits for them, and re-layouts  0.69 us (2%)
    ppermute x8, starting transfers between devices, swap(): lax.ppermute(value, ('grp', 'rep'), [(i, i ^ bit) for i in range(DEVICES)])  15 us
    all_to_all x1, blocking collectives, on_device(): lax.all_to_all(parcel, 'grp', 0, 0, axis_index_groups=SAME_X, tiled=True)  14.6 us
    ppermute x8, waiting for transfers between devices, swap(): lax.ppermute(value, ('grp', 'rep'), [(i, i ^ bit) for i in range(DEVICES)])  6.87 us
    pallas_call x1, Pallas kernels, spread(): rate_kernel(spread_kernel, 'spread', [float_rows(PHONON * COMPONENTS)] *...  2.75 us
    pallas_call x1, Pallas kernels, prepare(): rate_kernel(prepare_kernel, 'prepare', terms + [float_rows(8)], [HBM] * 3...  2.6 us
    pallas_call x1, Pallas kernels, forward(): rate_kernel(forward_kernel, 'forward', [float_rows(2 * ROWS)], [pl.BlockS...  1.85 us
  transfers between devices with their start and end apart: 8, of which 5 were waited for; matrix products, arithmetic and copies ran while one was open for 0% of the time, Pallas kernels for 6%

profile of v7, /device:TPU:1, one launch (start us, length us, event | category | flops | bytes accessed | tf_op | source)
XLA Modules:
  0.0 44.6 jit_solution(2163926025103392348)
XLA Ops:
  0.0 0.0 copy-start.2
  0.0 2.7 %spread.1 = (f32[384,128]{1,0:T(8,128)S(1)}, f32[384,128]{1,0:T(8,128)S(1)}) custom-call(s32[1,4]{1,0:T(1,128)} %bitcast.19, s32[4,5]{1,0:T(4,128)} %partner_hbm.5, f32[6,4,256]{2,1,0:T(4,128)} %bitcast.26, f32[4,5,256,256]{3,2,1,0:T(8,128)} %rates.3), custom_call_target="tpu_custom_call" | custom-call | flops 62914560 | bytes 10485760 | tf_op jit(solution)/shard_map/spread/pallas_call | solution.py:236
  2.8 3.6 %collective-permute-start = (f32[384,128]{1,0:T(8,128)S(1)}, f32[384,128]{1,0:T(8,128)S(1)}, u32[]{:S(2)}, u32[]{:S(2)}) collective-permute-start(f32[384,128]{1,0:T(8,128)S(1)} %get-tuple-element.15), channel_id=1, source_target_pairs={{0,1},{1,0},{2,3},{3,2},{4,5},{5,4},{6,7},{7,6},{8,9},{9,8},{10,11... | collective-permute-start | bytes 589832 | tf_op jit(solution)/shard_map/ppermute | solution.py:23
  6.3 0.0 copy-done.2
  6.4 1.0 %collective-permute-done = f32[384,128]{1,0:T(8,128)S(1)} collective-permute-done((f32[384,128]{1,0:T(8,128)S(1)}, f32[384,128]{1,0:T(8,128)S(1)}, u32[]{:S(2)}, u32[]{:S(2)}) %collective-permute-start) | collective-permute-done | bytes 196640 | tf_op jit(solution)/shard_map/ppermute | solution.py:23
  7.5 14.6 %all_to_all.5 = f32[16,24,128]{2,1,0:T(8,128)S(1)} all-to-all(f32[16,24,128]{2,1,0:T(8,128)S(1)} %fusion), channel_id=1, replica_groups={{0,4,8,12,16,20,24,28,128,132,136,140,144,148,152,156},{32,36,40,44,48,..., dimensions={0} | all-to-all | bytes 393216 | tf_op jit(solution)/shard_map/all_to_all | solution.py:278
  22.1 0.0 copy-start
  22.1 0.0 copy-start.1
  22.1 1.2 %collective-permute-start.1 = (f32[192,128]{1,0:T(8,128)S(1)}, f32[192,128]{1,0:T(8,128)S(1)}, u32[]{:S(2)}, u32[]{:S(2)}) collective-permute-start(f32[192,128]{1,0:T(8,128)S(1)} %bitcast_select_fusion.1), channel_id=1, source_target_pairs={{0,96},{1,97},{2,98},{3,99},{4,100},{5,101},{6,102},{7,103},{8,104... | collective-permute-start | bytes 294920 | tf_op jit(solution)/shard_map/ppermute | solution.py:23
  23.4 2.6 %prepare.1 = (bf16[20,256,256]{2,1,0:T(8,128)(2,1)S(1)}, bf16[20,256,256]{2,1,0:T(8,128)(2,1)S(1)}, f32[8,128]{1,0:T(8,128)S(1)}) custom-call(s32[1,4]{1,0:T(1,128)} %bitcast.20, s32[4,5]{1,0:T(4,128)} %partner_hbm.5, f32[4,5,256,256]{3,2,1,0:T(8,128)} %rates.3), custom_call_target="tpu_custom_call" | custom-call | flops 62914560 | bytes 10485760 | tf_op jit(solution)/shard_map/prepare/pallas_call | solution.py:244
  26.0 2.8 %collective-permute-start.3 = (f32[8,128]{1,0:T(8,128)S(1)}, f32[8,128]{1,0:T(8,128)S(1)}, u32[]{:S(2)}, u32[]{:S(2)}) collective-permute-start(f32[8,128]{1,0:T(8,128)S(1)} %get-tuple-element.18), channel_id=1, source_target_pairs={{0,1},{1,0},{2,3},{3,2},{4,5},{5,4},{6,7},{7,6},{8,9},{9,8},{10,11... | collective-permute-start | bytes 12296 | tf_op jit(solution)/shard_map/ppermute | solution.py:23
  28.8 0.0 collective-permute-done.1
  28.8 0.1 collective-permute-start.2
  29.0 1.8 %collective-permute-start.5 = (f32[24,128]{1,0:T(8,128)S(1)}, f32[24,128]{1,0:T(8,128)S(1)}, u32[]{:S(2)}, u32[]{:S(2)}) collective-permute-start(f32[24,128]{1,0:T(8,128)S(1)} %slice_add_fusion), channel_id=1, source_target_pairs={{0,160},{1,161},{2,162},{3,163},{4,164},{5,165},{6,166},{7,167},{8... | collective-permute-start | bytes 36872 | tf_op jit(solution)/shard_map/ppermute | solution.py:23
  30.8 1.6 %collective-permute-done.2 = f32[192,128]{1,0:T(8,128)S(1)} collective-permute-done((f32[192,128]{1,0:T(8,128)S(1)}, f32[192,128]{1,0:T(8,128)S(1)}, u32[]{:S(2)}, u32[]{:S(2)}) %collective-permute-start.2) | collective-permute-done | bytes 98336 | tf_op jit(solution)/shard_map/ppermute | solution.py:23
  32.4 0.0 collective-permute-done.3
  32.5 2.6 %collective-permute-start.4 = (f32[384,128]{1,0:T(8,128)S(1)}, f32[384,128]{1,0:T(8,128)S(1)}, u32[]{:S(2)}, u32[]{:S(2)}) collective-permute-start(f32[384,128]{1,0:T(8,128)S(1)} %pad_maximum_fusion.mine), channel_id=1, source_target_pairs={{0,1},{1,0},{2,3},{3,2},{4,5},{5,4},{6,7},{7,6},{8,9},{9,8},{10,11... | collective-permute-start | bytes 589832 | tf_op jit(solution)/shard_map/ppermute | solution.py:23
  35.1 0.0 collective-permute-done.5
  35.1 1.1 %collective-permute-done.4.other = f32[384,128]{1,0:T(8,128)S(1)} collective-permute-done((f32[384,128]{1,0:T(8,128)S(1)}, f32[384,128]{1,0:T(8,128)S(1)}, u32[]{:S(2)}, u32[]{:S(2)}) %collective-permute-start.4) | collective-permute-done | bytes 196640 | tf_op jit(solution)/shard_map/ppermute | solution.py:23
  36.2 0.0 copy-done
  36.2 0.0 copy-done.1
  36.2 0.0 copy-start.3
  36.2 0.0 copy-start.4
  36.2 1.8 %forward.1 = f32[48,128]{1,0:T(8,128)S(1)} custom-call(s32[1,4]{1,0:T(1,128)S(1)} %bitcast.21, s32[4,5]{1,0:T(4,128)S(1)} %copy-done, f32[384,128]{1,0:T(8,128)S(1)} %pad_maximum_fusion.mine, f32[384,128]{1,0:T(8,128)S(1)} %collective-permute-done.4.other, bf16[20,256,256]{2,1,0:T(8,128)(2,1)S(1)} %get-tuple-element.20.high_ref, ...), custom_call_target="tpu_custom_call" | custom-call | flops 62914560 | bytes 10485760 | tf_op jit(solution)/shard_map/forward/pallas_call | solution.py:251
  38.0 0.9 %collective-permute-start.6 = (f32[48,128]{1,0:T(8,128)S(1)}, f32[48,128]{1,0:T(8,128)S(1)}, u32[]{:S(2)}, u32[]{:S(2)}) collective-permute-start(f32[48,128]{1,0:T(8,128)S(1)} %forward.1), channel_id=1, source_target_pairs={{0,1},{1,0},{2,3},{3,2},{4,5},{5,4},{6,7},{7,6},{8,9},{9,8},{10,11... | collective-permute-start | bytes 73736 | tf_op jit(solution)/shard_map/ppermute | solution.py:23
  38.9 0.8 %collective-permute-done.6 = f32[48,128]{1,0:T(8,128)S(1)} collective-permute-done((f32[48,128]{1,0:T(8,128)S(1)}, f32[48,128]{1,0:T(8,128)S(1)}, u32[]{:S(2)}, u32[]{:S(2)}) %collective-permute-start.6) | collective-permute-done | bytes 24608 | tf_op jit(solution)/shard_map/ppermute | solution.py:23
  39.8 1.9 %collective-permute-start.7 = (f32[48,128]{1,0:T(8,128)S(1)}, f32[48,128]{1,0:T(8,128)S(1)}, u32[]{:S(2)}, u32[]{:S(2)}) collective-permute-start(f32[48,128]{1,0:T(8,128)S(1)} %add.54), channel_id=1, source_target_pairs={{0,2},{1,3},{2,0},{3,1},{4,6},{5,7},{6,4},{7,5},{8,10},{9,11},{10,... | collective-permute-start | bytes 73736 | tf_op jit(solution)/shard_map/ppermute | solution.py:23
  41.6 2.3 %collective-permute-done.7 = f32[48,128]{1,0:T(8,128)S(1)} collective-permute-done((f32[48,128]{1,0:T(8,128)S(1)}, f32[48,128]{1,0:T(8,128)S(1)}, u32[]{:S(2)}, u32[]{:S(2)}) %collective-permute-start.7) | collective-permute-done | bytes 24608 | tf_op jit(solution)/shard_map/ppermute | solution.py:23
  44.0 0.0 copy-done.3
  44.0 0.0 copy-done.4
  44.0 0.6 %copy.10 = f32[4,6,256]{2,0,1:T(4,128)} copy(f32[4,6,256]{2,1,0:T(8,128)S(1)} %fusion.2) | data formatting | bytes 49152 | tf_op jit(solution)/shard_map/transpose | solution.py:301
  (20 shorter events, 0.2 us)
Async XLA Ops:
  0.0 6.3 %copy-start.2 = (f32[4,6,256]{2,0,1:T(4,128)S(1)}, f32[4,6,256]{2,0,1:T(4,128)}, u32[]{:S(2)}) copy-start(f32[4,6,256]{2,0,1:T(4,128)} %param.6) | copy-start | bytes 73732
  2.8 4.6 %collective-permute-start = (f32[384,128]{1,0:T(8,128)S(1)}, f32[384,128]{1,0:T(8,128)S(1)}, u32[]{:S(2)}, u32[]{:S(2)}) collective-permute-start(f32[384,128]{1,0:T(8,128)S(1)} %get-tuple-element.15), channel_id=1, source_target_pairs={{0,1},{1,0},{2,3},{3,2},{4,5},{5,4},{6,7},{7,6},{8,9},{9,8},{10,11... | collective-permute-start | bytes 589832 | tf_op jit(solution)/shard_map/ppermute | solution.py:23
  22.1 14.1 %copy-start = (s32[4,5]{1,0:T(4,128)S(1)}, s32[4,5]{1,0:T(4,128)}, u32[]{:S(2)}) copy-start(s32[4,5]{1,0:T(4,128)} %partner_hbm.5) | copy-start | bytes 244
  22.1 14.0 %copy-start.1 = (s32[4,1]{0,1:T(1,128)S(1)}, s32[4,1]{0,1:T(1,128)}, u32[]{:S(2)}) copy-start(s32[4,1]{0,1:T(1,128)} %param.11) | copy-start | bytes 52
  22.1 6.7 %collective-permute-start.1 = (f32[192,128]{1,0:T(8,128)S(1)}, f32[192,128]{1,0:T(8,128)S(1)}, u32[]{:S(2)}, u32[]{:S(2)}) collective-permute-start(f32[192,128]{1,0:T(8,128)S(1)} %bitcast_select_fusion.1), channel_id=1, source_target_pairs={{0,96},{1,97},{2,98},{3,99},{4,100},{5,101},{6,102},{7,103},{8,104... | collective-permute-start | bytes 294920 | tf_op jit(solution)/shard_map/ppermute | solution.py:23
  26.0 6.5 %collective-permute-start.3 = (f32[8,128]{1,0:T(8,128)S(1)}, f32[8,128]{1,0:T(8,128)S(1)}, u32[]{:S(2)}, u32[]{:S(2)}) collective-permute-start(f32[8,128]{1,0:T(8,128)S(1)} %get-tuple-element.18), channel_id=1, source_target_pairs={{0,1},{1,0},{2,3},{3,2},{4,5},{5,4},{6,7},{7,6},{8,9},{9,8},{10,11... | collective-permute-start | bytes 12296 | tf_op jit(solution)/shard_map/ppermute | solution.py:23
  28.8 3.6 %collective-permute-start.2 = (f32[192,128]{1,0:T(8,128)S(1)}, f32[192,128]{1,0:T(8,128)S(1)}, u32[]{:S(2)}, u32[]{:S(2)}) collective-permute-start(f32[192,128]{1,0:T(8,128)S(1)} %bitcast_select_fusion), channel_id=1, source_target_pairs={{0,32},{1,33},{2,34},{3,35},{4,36},{5,37},{6,38},{7,39},{8,40},{9,... | collective-permute-start | bytes 294920 | tf_op jit(solution)/shard_map/ppermute | solution.py:23
  29.0 6.1 %collective-permute-start.5 = (f32[24,128]{1,0:T(8,128)S(1)}, f32[24,128]{1,0:T(8,128)S(1)}, u32[]{:S(2)}, u32[]{:S(2)}) collective-permute-start(f32[24,128]{1,0:T(8,128)S(1)} %slice_add_fusion), channel_id=1, source_target_pairs={{0,160},{1,161},{2,162},{3,163},{4,164},{5,165},{6,166},{7,167},{8... | collective-permute-start | bytes 36872 | tf_op jit(solution)/shard_map/ppermute | solution.py:23
  32.5 3.7 %collective-permute-start.4 = (f32[384,128]{1,0:T(8,128)S(1)}, f32[384,128]{1,0:T(8,128)S(1)}, u32[]{:S(2)}, u32[]{:S(2)}) collective-permute-start(f32[384,128]{1,0:T(8,128)S(1)} %pad_maximum_fusion.mine), channel_id=1, source_target_pairs={{0,1},{1,0},{2,3},{3,2},{4,5},{5,4},{6,7},{7,6},{8,9},{9,8},{10,11... | collective-permute-start | bytes 589832 | tf_op jit(solution)/shard_map/ppermute | solution.py:23
  36.2 7.8 %copy-start.3 = (f32[4,6,256]{2,0,1:T(4,128)S(1)}, f32[4,6,256]{2,0,1:T(4,128)}, u32[]{:S(2)}) copy-start(f32[4,6,256]{2,0,1:T(4,128)} %param.7) | copy-start | bytes 73732
  36.2 7.8 %copy-start.4 = (f32[4,256]{1,0:T(4,128)S(1)}, f32[4,256]{1,0:T(4,128)}, u32[]{:S(2)}) copy-start(f32[4,256]{1,0:T(4,128)} %param.8) | copy-start | bytes 12292
  38.0 1.7 %collective-permute-start.6 = (f32[48,128]{1,0:T(8,128)S(1)}, f32[48,128]{1,0:T(8,128)S(1)}, u32[]{:S(2)}, u32[]{:S(2)}) collective-permute-start(f32[48,128]{1,0:T(8,128)S(1)} %forward.1), channel_id=1, source_target_pairs={{0,1},{1,0},{2,3},{3,2},{4,5},{5,4},{6,7},{7,6},{8,9},{9,8},{10,11... | collective-permute-start | bytes 73736 | tf_op jit(solution)/shard_map/ppermute | solution.py:23
  39.8 4.2 %collective-permute-start.7 = (f32[48,128]{1,0:T(8,128)S(1)}, f32[48,128]{1,0:T(8,128)S(1)}, u32[]{:S(2)}, u32[]{:S(2)}) collective-permute-start(f32[48,128]{1,0:T(8,128)S(1)} %add.54), channel_id=1, source_target_pairs={{0,2},{1,3},{2,0},{3,1},{4,6},{5,7},{6,4},{7,5},{8,10},{9,11},{10,... | collective-permute-start | bytes 73736 | tf_op jit(solution)/shard_map/ppermute | solution.py:23
